TPU v7x, 256 devices: a whole 4x4x8 slice. The times are simulated.
256 devices in a mesh: dp: 32 (over x, y, core), tensor: 4 (over z_lo), pre: 2 (over z_hi).
Axes of the slice: x: 4, y: 4, z: 8 (z_hi: 2, z_lo: 4; z = z_hi * 4 + z_lo), core: 2. Of those that a mesh axis runs over, the one named last changes fastest.
Arguments:
- acts: bfloat16 [4096, 8192], P('dp', ('tensor', 'pre')), may hold values from -6 to 6
- grad_out: bfloat16 [4096, 2048], P('dp', ('tensor', 'pre')), may hold values from -0.09375 to 0.09375
- owners: int32 [16, 16], P(None, ('tensor', 'pre')), may hold values from 0 to 31, as said below
- left_stats: float32 [32, 2, 512, 4096], P('dp', None, None, ('tensor', 'pre')), may hold values from -0.12 to 256, as said below
- right_stats: float32 [32, 2, 128, 1024], P('dp', None, None, ('tensor', 'pre')), may hold values from -1.9 to 1024, as said below
Outputs:
- new_left: float32 [32, 2, 512, 4096], P('dp', None, None, ('tensor', 'pre'))
- new_right: float32 [32, 2, 128, 1024], P('dp', None, None, ('tensor', 'pre'))
- update: float32 [8192, 2048], P('dp', ('tensor', 'pre'))
Inputs may be any that keep to these rules, and one draw needn't show every extreme that they name: `owners`: within every head group no owner holds more than 2 blocks, and some owner holds exactly 2. `left_stats`: Symmetric, with every diagonal entry larger than the sum of magnitudes of its row's other entries. `right_stats`: Symmetric, with every diagonal entry larger than the sum of magnitudes of its row's other entries.
All inputs are finite; a program needn't handle non-finite values.
Results may differ from a plain program's by a relative error of at most 0.0003.
Values may be sent and summed in bfloat16 or wider, within the bound.
A program may use at most 128 MiB of HBM per device.

v0:
```python
import jax
import jax.numpy as jnp
from jax import lax
from jax.sharding import PartitionSpec as P

D = 8192
ITERS = 3


decay_rate = 0.95
graft_eps = 1e-06


def matmul_hi(left, right):
    return jnp.einsum("...ij,...jk->...ik", left, right, precision=lax.Precision.HIGHEST)


def flip_last(matrix):
    return jnp.swapaxes(matrix, -1, -2)


def inverse_root(matrix):
    mat_order = matrix.shape[-1]
    identity = jnp.eye(mat_order, dtype=jnp.float32)
    frob_norm = jnp.sqrt(jnp.sum(matrix * matrix, axis=(-2, -1), keepdims=True))
    scaling = 2.5 / frob_norm
    power_term = scaling * matrix
    root_term = jnp.sqrt(jnp.sqrt(scaling)) * identity
    for repeat in range(ITERS):
        factor = (5.0 * identity - power_term) * 0.25
        root_term = matmul_hi(root_term, factor)
        square = matmul_hi(factor, factor)
        fourth = matmul_hi(square, square)
        power_term = matmul_hi(fourth, power_term)
    return root_term


def slots_of(owner_of):
    block_ids = jnp.arange(owner_of.shape[0], dtype=jnp.int32)
    same_owner = owner_of[:, None] == owner_of[None, :]
    earlier = block_ids[None, :] < block_ids[:, None]
    return jnp.sum((same_owner & earlier).astype(jnp.int32), axis=1)


def precondition(blocks, left_new, right_new):
    left_root = inverse_root(left_new)
    right_root = inverse_root(right_new)
    shaped = matmul_hi(matmul_hi(left_root, blocks), right_root)
    grad_mean = jnp.mean(blocks * blocks, axis=(-2, -1), keepdims=True)
    shaped_mean = jnp.mean(shaped * shaped, axis=(-2, -1), keepdims=True)
    return shaped * jnp.sqrt(grad_mean / (shaped_mean + graft_eps))


def on_device(acts, grad_out, owners, left_stats, right_stats):
    devices = lax.axis_size("dp")
    my_index = lax.axis_index("dp")
    capacity = left_stats.shape[1]
    block_size = left_stats.shape[2]
    head_dim = right_stats.shape[2]
    col_blocks = owners.shape[1]
    count_blocks = owners.shape[0] * col_blocks
    rows_dev = D // devices
    piece_rows = min(block_size, rows_dev)
    per_block = block_size // piece_rows
    per_dev = rows_dev // piece_rows
    piece_count = D // piece_rows
    owner_of = owners.reshape(count_blocks)
    slot_of = slots_of(owner_of)
    block_ids = jnp.arange(count_blocks, dtype=jnp.int32)
    row_of = block_ids // col_blocks
    col_of = block_ids % col_blocks
    col_hot = (col_of[:, None] == jnp.arange(col_blocks, dtype=jnp.int32)[None, :]).astype(
        jnp.float32
    )
    owner_hot = (owner_of[:, None] == jnp.arange(devices, dtype=jnp.int32)[None, :]).astype(
        jnp.float32
    )
    slot_hot = (slot_of[:, None] == jnp.arange(capacity, dtype=jnp.int32)[None, :]).astype(
        jnp.float32
    )
    is_mine = (owner_of == my_index).astype(jnp.int32)
    slot_block = jnp.transpose(slot_hot.astype(jnp.int32) * is_mine[:, None])
    slot_valid = jnp.sum(slot_block, axis=1).astype(jnp.float32)
    slot_row = jnp.sum(slot_block * row_of[None, :], axis=1)
    slot_cols = jnp.dot(slot_block.astype(jnp.float32), col_hot)
    partial_grads = lax.dot_general(
        lax.all_gather(acts, ("tensor", "pre"), axis=1, tiled=True),
        grad_out,
        (((0,), (0,)), ((), ())),
        preferred_element_type=jnp.float32,
    )
    summed = lax.psum_scatter(partial_grads, "dp", scatter_dimension=0, tiled=True)
    local_rows = summed.reshape(per_dev, piece_rows, col_blocks, head_dim)
    holds = (my_index // per_block == row_of).astype(jnp.float32)
    local_index = jnp.zeros_like(row_of)
    local_hot = (local_index[:, None] == jnp.arange(per_dev, dtype=jnp.int32)[None, :]).astype(
        jnp.float32
    )
    pieces = jnp.einsum(
        "kl,kc,lpch->kph", local_hot, col_hot, local_rows, precision=lax.Precision.HIGHEST
    )
    weight = owner_hot[:, :, None] * slot_hot[:, None, :] * holds[:, None, None]
    outbox = jnp.einsum("kos,kph->osph", weight, pieces, precision=lax.Precision.HIGHEST)
    incoming = lax.all_to_all(outbox, "dp", split_axis=0, concat_axis=0, tiled=True)
    source = (
        slot_row[:, None] * per_block + jnp.arange(per_block, dtype=jnp.int32)[None, :]
    ) // per_dev
    source_hot = (source[:, :, None] == jnp.arange(devices, dtype=jnp.int32)[None, None, :]).astype(
        jnp.float32
    ) * slot_valid[:, None, None]
    gathered = jnp.einsum(
        "sjn,nsph->sjph", source_hot, incoming, precision=lax.Precision.HIGHEST
    ).reshape(capacity, block_size, head_dim)
    left_new = decay_rate * left_stats[0] + matmul_hi(gathered, flip_last(gathered))
    right_new = decay_rate * right_stats[0] + matmul_hi(flip_last(gathered), gathered)
    shaped = precondition(gathered, left_new, right_new)
    shaped_pieces = shaped.reshape(capacity, per_block, piece_rows, head_dim)
    global_piece = slot_row[:, None] * per_block + jnp.arange(per_block, dtype=jnp.int32)[None, :]
    piece_hot = (
        global_piece[:, :, None] == jnp.arange(piece_count, dtype=jnp.int32)[None, None, :]
    ).astype(jnp.float32) * slot_valid[:, None, None]
    return_box = jnp.einsum(
        "sjg,sc,sjph->gpch", piece_hot, slot_cols, shaped_pieces, precision=lax.Precision.HIGHEST
    )
    return_box = return_box.reshape(devices, rows_dev, col_blocks * head_dim)
    arrived = lax.all_to_all(return_box, "dp", split_axis=0, concat_axis=0, tiled=True)
    update = jnp.sum(arrived, axis=0)
    return (left_new[None], right_new[None], update)


def solution(mesh):
    in_specs = (
        P("dp", ("tensor", "pre")),
        P("dp", ("tensor", "pre")),
        P(None, ("tensor", "pre")),
        P("dp", None, None, ("tensor", "pre")),
        P("dp", None, None, ("tensor", "pre")),
    )
    out_specs = (
        P("dp", None, None, ("tensor", "pre")),
        P("dp", None, None, ("tensor", "pre")),
        P("dp", ("tensor", "pre")),
    )
    return jax.shard_map(
        on_device, mesh=mesh, in_specs=in_specs, out_specs=out_specs, check_vma=False
    )
```

profile of v0, /device:TPU:1, one launch (start us, length us, event | category | flops | bytes accessed | tf_op | source)
XLA Modules:
  0.0 611.8 jit_solution(4984276240359205490)
XLA Ops:
  7.2 0.7 all-gather.2.cloned.1.call-update
  8.0 120.2 %all-gather.2.cloned.1.call-done = bf16[128,8192]{1,0:T(8,128)(2,1)} async-done(((bf16[128,1024]{1,0:T(8,128)(2,1)}), bf16[128,8192]{1,0:T(8,128)(2,1)}) %all-gather.2.cloned.1.call-update) | async-done | bytes 2097168 | tf_op jit(solution)/shard_map/all_gather | solution.py:87
  128.1 6.1 fusion.100
  134.3 0.6 copy-done.6
  135.2 98.5 %reduce-scatter.2.cloned.1.call-done = f32[256,256]{1,0:T(8,128)} async-done(((f32[8192,256]{1,0:T(8,128)}), f32[256,256]{1,0:T(8,128)}) %reduce-scatter.2.cloned.1.call-update) | async-done | bytes 262160 | tf_op jit(solution)/shard_map/reduce_scatter | solution.py:92
  233.7 1.1 reshape.219
  234.8 1.9 fusion.70
  236.7 7.0 %fusion.7 = f32[32,2,256,128]{3,0,2,1:T(8,128)S(1)} fusion(f32[32,256,128]{2,0,1:T(8,128)S(1)} %fusion.70, f32[32]{0:T(128)S(1)} %compare_convert_fusion, f32[32,2]{0,1:T(2,128)S(1)} %compare_convert_fusion.1, f32[32,32]{0,1:T(8,128)S(1)} %fusion.68), kind=kOutput, calls=%fused_computation.5 | convolution fusion | flops 805310464 | bytes 12587392 | tf_op jit(solution)/shard_map/kos,kph->osph/dot_general | solution.py:103
  243.7 8.2 %copy.25 = f32[32,2,256,128]{3,2,1,0:T(8,128)} copy(f32[32,2,256,128]{3,0,2,1:T(8,128)S(1)} %fusion.7) | data formatting | bytes 16777216 | tf_op jit(solution)/shard_map/kos,kph->osph/dot_general | solution.py:103
  251.9 7.4 %all-to-all-start = ((f32[32,2,256,128]{3,2,1,0:T(8,128)}), f32[32,2,256,128]{3,2,1,0:T(8,128)}, u32[]{:S(2)}, u32[]{:S(2)}) async-start(f32[32,2,256,128]{3,2,1,0:T(8,128)} %copy.25), calls=%async_computation.1 | async-start | bytes 16777216 | tf_op jit(solution)/shard_map/all_to_all | solution.py:104
  260.1 107.8 %all-to-all-done = f32[32,2,256,128]{3,2,1,0:T(8,128)} async-done(((f32[32,2,256,128]{3,2,1,0:T(8,128)}), f32[32,2,256,128]{3,2,1,0:T(8,128)}, u32[]{:S(2)}, u32[]{:S(2)}) %all-to-all-start) | async-done | bytes 8388640 | tf_op jit(solution)/shard_map/all_to_all | solution.py:104
  367.9 12.7 %multiply_reduce_fusion.2 = (f32[2]{0:T(128)S(1)}, f32[2,2,256,128]{3,1,2,0:T(2,128)S(1)}) fusion(f32[32,2,256,128]{3,2,1,0:T(8,128)} %all-to-all-done, f32[2]{0:T(128)S(1)} %convert_element_type.74, s32[2,2]{1,0:T(2,128)S(1)} %iota_add_fusion), kind=kOutput, calls=%fused_computation.46 | convolution fusion | flops 50594048 | bytes 8912928 | tf_op jit(solution)/shard_map/sjn,nsph->sjph/dot_general | solution.py:111
  380.7 1.1 multiply_reduce_fusion.3
  381.8 0.4 fusion.45
  384.3 2.1 multiply_reduce_fusion
  386.4 4.0 fusion.18
  390.4 3.5 fusion.101
  393.9 4.1 fusion.14
  398.0 3.7 fusion.16
  401.8 3.5 fusion.102
  405.3 3.5 fusion.103
  408.8 4.0 fusion.12
  412.9 3.7 fusion.17
  416.6 3.7 fusion.9
  420.3 1.9 fusion.104
  422.5 0.9 multiply_reduce_fusion.1
  423.5 7.0 %fusion.37 = f32[2,256,128,32]{2,3,1,0:T(8,128)S(1)} fusion(f32[2,2,256,128]{3,2,1,0:T(8,128)S(1)} %bitcast.71, f32[2]{0:T(128)S(1)} %convert_element_type.74, s32[2,2]{1,0:T(2,128)S(1)} %iota_add_fusion), kind=kOutput, calls=%fused_computation.43 | convolution fusion | flops 50331904 | bytes 8912920 | tf_op jit(solution)/shard_map/sjg,sc,sjph->gpch/dot_general | solution.py:122
  430.5 32.3 %fusion.4 = f32[32,256,2,128]{3,2,0,1:T(2,128)} fusion(f32[2,2,1,1]{0,1,3,2:T(2,128)S(1)} %convolution_bitcast_fusion, f32[2,256,128,32]{2,3,1,0:T(8,128)S(1)} %fusion.37), kind=kOutput, calls=%fused_computation.4 | convolution fusion | flops 50331648 | bytes 16777232 | tf_op jit(solution)/shard_map/sjg,sc,sjph->gpch/dot_general | solution.py:122
  462.9 11.8 %reshape.222 = f32[32,256,256]{2,0,1:T(8,128)} reshape(f32[32,256,2,128]{3,2,0,1:T(2,128)} %fusion.4) | data formatting | bytes 16777216 | tf_op jit(solution)/shard_map/reshape | solution.py:125
  474.7 8.2 %copy.32 = f32[32,256,256]{2,1,0:T(8,128)S(1)} copy(f32[32,256,256]{2,0,1:T(8,128)} %reshape.222) | data formatting | bytes 16777216 | tf_op jit(solution)/shard_map/reshape | solution.py:125
  482.9 116.9 %all_to_all.10 = f32[32,256,256]{2,1,0:T(8,128)} all-to-all(f32[32,256,256]{2,1,0:T(8,128)S(1)} %copy.32), channel_id=1, replica_groups=mesh['dp'=32,'tensor'=4,'pre'=2] {'dp'}, dimensions={0} | all-to-all | bytes 16777216 | tf_op jit(solution)/shard_map/all_to_all | solution.py:126
  599.8 4.7 reduce_sum.79
  (48 shorter events, 3.6 us)
Async XLA Ops:
  7.2 121.0 %copy-start = (bf16[128,256]{1,0:T(8,128)(2,1)S(1)}, bf16[128,256]{1,0:T(8,128)(2,1)}, u32[]{:S(2)}) copy-start(bf16[128,256]{1,0:T(8,128)(2,1)} %param.6) | copy-start | bytes 196612
  7.2 121.0 %all-gather.2.cloned.1.call-start = ((), (), s32[]{:S(2)}) async-start(), calls=%async_computation.3 | async-start | bytes 2359296 | tf_op jit(solution)/shard_map/all_gather | solution.py:87
  7.9 225.8 %reduce-scatter.2.cloned.1.call-start = ((), (), s32[]{:S(2)}) async-start(), calls=%async_computation.4 | async-start | bytes 8650752 | tf_op jit(solution)/shard_map/reduce_scatter | solution.py:92
  134.2 0.7 copy-start.6
  251.9 116.0 %all-to-all-start = ((f32[32,2,256,128]{3,2,1,0:T(8,128)}), f32[32,2,256,128]{3,2,1,0:T(8,128)}, u32[]{:S(2)}, u32[]{:S(2)}) async-start(f32[32,2,256,128]{3,2,1,0:T(8,128)} %copy.25), calls=%async_computation.1 | async-start | bytes 16777216 | tf_op jit(solution)/shard_map/all_to_all | solution.py:104
  260.1 120.5 %copy-start.5 = (f32[1,2,128,128]{3,2,1,0:T(8,128)S(1)}, f32[1,2,128,128]{3,2,1,0:T(8,128)}, u32[]{:S(2)}) copy-start(f32[1,2,128,128]{3,2,1,0:T(8,128)} %param.9) | copy-start | bytes 393220
  380.7 3.6 copy-start.4
  381.8 4.6 copy-start.3
  386.4 22.4 %copy-start.2 = (f32[2,512,512]{2,1,0:T(8,128)}, f32[2,512,512]{2,1,0:T(8,128)S(1)}, u32[]{:S(2)}) copy-start(f32[2,512,512]{2,1,0:T(8,128)S(1)} %get-tuple-element.8) | copy-start | bytes 6291460
  599.8 4.7 copy-start.1
Sparse Core Ops, SparseCore 0:
  9.8 118.2 all-gather.1
  134.4 99.2 reduce-scatter.1
where the time goes:
time: 621 us; the launch traced here: 612 us
  waiting for transfers between devices  327 us (53%)
  blocking collectives  117 us (19%)
  matrix products  110 us (18%)
  local copies, waits for them, and re-layouts  30.2 us (5%)
  between operations  14.9 us (2%)
  starting transfers between devices  7.5 us (1%)
    all_gather x1, waiting for transfers between devices, on_device(): lax.all_gather(acts, ('tensor', 'pre'), axis=1, tiled=True)  120 us
    all_to_all x1, blocking collectives, on_device(): lax.all_to_all(return_box, 'dp', split_axis=0, concat_axis=0, tiled=True)  117 us
    all_to_all x1, waiting for transfers between devices, on_device(): lax.all_to_all(outbox, 'dp', split_axis=0, concat_axis=0, tiled=True)  108 us
    reduce_scatter x1, waiting for transfers between devices, on_device(): lax.psum_scatter(partial_grads, 'dp', scatter_dimension=0, tiled=True)  98.5 us
    dot_general x22, matrix products, matmul_hi(): jnp.einsum('...ij,...jk->...ik', left, right, precision=lax.Precision.HIG...  42.5 us
    dot_general x2, matrix products, on_device(): jnp.einsum('sjg,sc,sjph->gpch', piece_hot, slot_cols, shaped_pieces, prec...  39.3 us
    reshape x2, local copies, waits for them, and re-layouts, on_device(): return_box = return_box.reshape(devices, rows_dev, col_blocks * head_dim)  20 us
    dot_general x1, matrix products, on_device(): jnp.einsum('sjn,nsph->sjph', source_hot, incoming, precision=lax.Precisio...  12.7 us
  transfers between devices with their start and end apart: 3, of which 3 were waited for; matrix products, arithmetic and copies ran while one was open for 0% of the time, Pallas kernels for 0%

commit v1 on v0

v1 whole, which is shorter than its diff:
```python
import jax
import jax.numpy as jnp
from jax import lax
from jax.experimental import pallas as pl
from jax.experimental.pallas import tpu as pltpu
from jax.sharding import PartitionSpec as P

MESH = pl.DeviceIdType.MESH
N_DP = 32
N_Z = 8
CHUNKS = 4
PER = N_DP // CHUNKS
decay_rate = 0.95
graft_eps = 1e-06


def split(x):
    hi = x.astype(jnp.bfloat16)
    lo = (x - hi.astype(jnp.float32)).astype(jnp.bfloat16)
    return hi, lo


def dot(a, b, dims):
    return lax.dot_general(a, b, (dims, ((), ())), preferred_element_type=jnp.float32)


def mul(a, b, dims=((1,), (0,))):
    return dot(a[0], b[0], dims) + (dot(a[0], b[1], dims) + dot(a[1], b[0], dims))


def eye_of(n):
    rows = lax.broadcasted_iota(jnp.int32, (n, n), 0)
    cols = lax.broadcasted_iota(jnp.int32, (n, n), 1)
    return jnp.where(rows == cols, 1.25, 0.0).astype(jnp.float32)


def total(x):
    return jnp.sum(jnp.sum(x, axis=0, keepdims=True), axis=1, keepdims=True)


def precondition(g, left, right):
    eye_l = eye_of(512)
    eye_r = eye_of(128)
    z_l = 2.5 * lax.rsqrt(total(left * left))
    z_r = 2.5 * lax.rsqrt(total(right * right))

    m = z_l * left
    ms = split(m)
    fs = split(eye_l - 0.25 * m)
    ss = split(mul(fs, fs))
    qs = split(mul(ss, ss))
    m2s = split(mul(qs, ms))

    n = z_r * right
    ns = split(n)
    f = eye_r - 0.25 * n
    es = split(f)
    ts = split(mul(es, es))
    us = split(mul(ts, ts))
    n2 = mul(us, ns)
    n2s = split(n2)
    f2 = split(eye_r - 0.25 * n2)
    r12 = split(mul(es, f2))
    ts = split(mul(f2, f2))
    us = split(mul(ts, ts))
    n3 = mul(us, n2s)
    root_r = split(mul(r12, split(eye_r - 0.25 * n3)))

    v1 = 1.25 * g - 0.25 * mul(ms, split(g))
    f2 = split(eye_l - 0.25 * (m2s[0].astype(jnp.float32) + m2s[1].astype(jnp.float32)))
    s2 = split(mul(f2, f2))
    v2 = 1.25 * v1 - 0.25 * mul(m2s, split(v1))
    w = mul(m2s, split(v2))
    w = mul(s2, split(w))
    w = mul(s2, split(w))
    v3 = 1.25 * v2 - 0.25 * w
    shaped = mul(split(v3), root_r)
    shaped = shaped * (jnp.sqrt(jnp.sqrt(z_l)) * jnp.sqrt(jnp.sqrt(z_r)))
    count = 1.0 / (512 * 128)
    grad_mean = total(g * g) * count
    shaped_mean = total(shaped * shaped) * count
    return shaped * jnp.sqrt(grad_mean / (shaped_mean + graft_eps))


def kernel(
    inv, pos, acts_hbm, go_hbm, left_hbm, right_hbm,
    new_left_hbm, new_right_ref, update_ref,
    acts_v, out_a, a_buf, go_buf, left_v, right_v, nl_v, pieces, outbox, inbox,
    retbox, rinbox, fbox, finbox,
    in_sem, out_sem, a_send, a_recv, go_send, go_recv, fw_send,
    zr_send, zr_recv, zl_send, zl_recv,
    d_send, d_recv, r_send, r_recv, f_send, f_recv,
):
    me = lax.axis_index("dp")
    tensor = lax.axis_index("tensor")
    pre = lax.axis_index("pre")
    z = pre * 4 + tensor
    partner = me + 1 - 2 * (me % 2)

    load_acts = pltpu.make_async_copy(acts_hbm, acts_v, in_sem.at[0])
    load_acts.start()
    load_go = pltpu.make_async_copy(go_hbm, go_buf.at[me], in_sem.at[1])
    load_go.start()
    load_left = pltpu.make_async_copy(left_hbm.at[0], left_v, in_sem.at[2])
    load_left.start()
    load_right = pltpu.make_async_copy(right_hbm.at[0], right_v, in_sem.at[3])
    load_right.start()

    def z_dev(zz):
        zz = lax.rem(zz + N_Z, N_Z)
        return {"tensor": lax.rem(zz, 4), "pre": zz // 4}

    def slice_of(zz):
        zz = lax.rem(zz + N_Z, N_Z)
        return lax.rem(zz, 4) * 2 + zz // 4

    barrier = pltpu.get_barrier_semaphore()

    def greet(i, carry):
        pl.semaphore_signal(
            barrier, inc=1, device_id={"dp": lax.rem(me + i, N_DP)}, device_id_type=MESH
        )
        return carry

    lax.fori_loop(1, N_DP, greet, 0)
    for step in (1, -1):
        pl.semaphore_signal(barrier, inc=1, device_id=z_dev(z + step), device_id_type=MESH)

    load_acts.wait()
    for c in range(8):
        turned = acts_v[:, c * 128 : (c + 1) * 128].T
        for e in range(8):
            row = c * 128 + e * 16
            out_a[(row % 512) // 16, (row // 512) * 16 : (row // 512) * 16 + 16] = turned[
                e * 16 : e * 16 + 16
            ]
    mine = slice_of(z)
    a_buf[mine, me] = out_a[me]

    pl.semaphore_wait(barrier, N_DP + 1)

    def send_a(i, carry):
        peer = lax.rem(me + i, N_DP)
        pltpu.make_async_remote_copy(
            src_ref=out_a.at[peer], dst_ref=a_buf.at[mine, me],
            send_sem=a_send.at[i], recv_sem=a_recv.at[me],
            device_id={"dp": peer}, device_id_type=MESH,
        ).start()
        return carry

    lax.fori_loop(1, N_DP, send_a, 0)

    load_go.wait()

    def go_copy(i):
        peer = lax.rem(me + 2 * i, N_DP)
        return pltpu.make_async_remote_copy(
            src_ref=go_buf.at[me], dst_ref=go_buf.at[me],
            send_sem=go_send.at[i], recv_sem=go_recv.at[me],
            device_id={"dp": peer}, device_id_type=MESH,
        )

    def fw_copy(i, src):
        return pltpu.make_async_remote_copy(
            src_ref=go_buf.at[src], dst_ref=go_buf.at[src],
            send_sem=fw_send.at[i], recv_sem=go_recv.at[src],
            device_id={"dp": partner}, device_id_type=MESH,
        )

    def send_go(i, carry):
        go_copy(i).start()
        return carry

    fw_copy(0, me).start()
    lax.fori_loop(1, N_DP // 2, send_go, 0)

    def ring(step, chunk, way):
        sems = (zr_send, zr_recv) if way == 1 else (zl_send, zl_recv)
        ref = a_buf.at[slice_of(z - way * (step - 1)), pl.ds(chunk * PER, PER)]
        return pltpu.make_async_remote_copy(
            src_ref=ref, dst_ref=ref,
            send_sem=sems[0].at[step - 1, chunk], recv_sem=sems[1].at[step - 1, chunk],
            device_id=z_dev(z + way), device_id_type=MESH,
        )

    def arrived(step, chunk, way):
        sems = zr_recv if way == 1 else zl_recv
        ref = a_buf.at[slice_of(z - way * step), pl.ds(chunk * PER, PER)]
        pltpu.make_async_copy(ref, ref, sems.at[step - 1, chunk]).wait()

    def has(step, chunk, way):
        return step < 4 or (chunk < CHUNKS // 2) == (way == 1)

    def wait_a(i, carry):
        @pl.when(i != me)
        def _():
            ref = a_buf.at[mine, i]
            pltpu.make_async_copy(ref, ref, a_recv.at[i]).wait()

        return carry

    def wait_go(src):
        ref = go_buf.at[src]
        pltpu.make_async_copy(ref, ref, go_recv.at[src]).wait()

    def forward_go(i, carry):
        src = lax.rem(me + 2 * i, N_DP)
        wait_go(src)
        fw_copy(i, src).start()
        return carry

    for step in range(1, 5):
        for chunk in range(CHUNKS):
            if step == 1:
                lax.fori_loop(chunk * PER, (chunk + 1) * PER, wait_a, 0)
            for way in (1, -1):
                if step > 1:
                    arrived(step - 1, chunk, way)
                if has(step, chunk, way):
                    ring(step, chunk, way).start()
        if step == 3:
            lax.fori_loop(1, N_DP // 2, forward_go, 0)

    def wait_partner(i, carry):
        wait_go(2 * i + 1 - lax.rem(me, 2))
        return carry

    lax.fori_loop(0, N_DP // 2, wait_partner, 0)
    for chunk in range(CHUNKS):
        arrived(4, chunk, 1 if chunk < CHUNKS // 2 else -1)

    acc = jnp.zeros((256, 256), jnp.float32)
    for m in range(N_DP // 2):
        lhs = jnp.concatenate(
            [a_buf[:, 2 * m].reshape(256, 128), a_buf[:, 2 * m + 1].reshape(256, 128)], axis=1
        )
        acc = acc + jnp.dot(
            lhs, go_buf[2 * m : 2 * m + 2].reshape(256, 256), preferred_element_type=jnp.float32
        )
    for c in range(2):
        pieces[:, c] = acc[:, c * 128 : (c + 1) * 128].reshape(16, 16, 128)

    def fill(o):
        for s in range(2):
            block = inv[2 * o + s]
            used = jnp.maximum(block, 0)
            value = pieces[used // 2, lax.rem(used, 2)]
            outbox[o, s] = jnp.where(block >= 0, value, 0.0)

    def to_owner(i, carry):
        peer = lax.rem(me + i, N_DP)
        fill(peer)
        pltpu.make_async_remote_copy(
            src_ref=outbox.at[peer], dst_ref=inbox.at[me],
            send_sem=d_send.at[i], recv_sem=d_recv.at[me],
            device_id={"dp": peer}, device_id_type=MESH,
        ).start()
        return carry

    lax.fori_loop(1, N_DP, to_owner, 0)
    fill(me)
    inbox[me] = outbox[me]
    load_left.wait()
    load_right.wait()

    def wait_box(box, sem):
        def one(i, carry):
            @pl.when(i != me)
            def _():
                ref = box.at[i]
                pltpu.make_async_copy(ref, ref, sem.at[i]).wait()

            return carry

        lax.fori_loop(0, N_DP, one, 0)

    def wait_sent(box, sem):
        def one(i, carry):
            ref = box.at[0]
            pltpu.make_async_copy(ref, ref, sem.at[i]).wait()
            return carry

        lax.fori_loop(1, N_DP, one, 0)

    wait_box(inbox, d_recv)

    stores = []
    shaped = []
    for s in range(2):
        g = inbox[:, s].reshape(512, 128)
        gs = split(g)
        nl_v[s] = decay_rate * left_v[s] + mul(gs, gs, ((1,), (1,)))
        store = pltpu.make_async_copy(nl_v.at[s], new_left_hbm.at[0, s], out_sem.at[s])
        store.start()
        stores.append(store)
        new_right_ref[0, s] = decay_rate * right_v[s] + mul(gs, gs, ((0,), (0,)))
    for s in range(2):
        g = inbox[:, s].reshape(512, 128)
        shaped.append(precondition(g, nl_v[s], new_right_ref[0, s]))
    for s in range(2):
        for half in range(2):
            retbox[:, s, half] = shaped[s][half * 256 : (half + 1) * 256].reshape(N_DP, 8, 128)

    def send_back(i, carry):
        peer = lax.rem(me + i, N_DP)
        pltpu.make_async_remote_copy(
            src_ref=retbox.at[peer], dst_ref=rinbox.at[me],
            send_sem=r_send.at[i], recv_sem=r_recv.at[me],
            device_id={"dp": peer}, device_id_type=MESH,
        ).start()
        return carry

    lax.fori_loop(1, N_DP, send_back, 0)
    rinbox[me] = retbox[me]
    wait_box(rinbox, r_recv)

    def pick(d):
        for c in range(2):
            where = pos[(d // 2) * 2 + c]
            fbox[d, c] = rinbox[where // 2, lax.rem(where, 2), lax.rem(d, 2)]

    def to_holder(i, carry):
        peer = lax.rem(me + i, N_DP)
        pick(peer)
        pltpu.make_async_remote_copy(
            src_ref=fbox.at[peer], dst_ref=finbox.at[me],
            send_sem=f_send.at[i], recv_sem=f_recv.at[me],
            device_id={"dp": peer}, device_id_type=MESH,
        ).start()
        return carry

    lax.fori_loop(1, N_DP, to_holder, 0)
    pick(me)
    finbox[me] = fbox[me]

    wait_sent(out_a, a_send)
    wait_sent(outbox, d_send)
    wait_sent(retbox, r_send)
    go_ref = go_buf.at[0]

    def wait_go_sent(i, carry):
        pltpu.make_async_copy(go_ref, go_ref, go_send.at[i]).wait()
        pltpu.make_async_copy(go_ref, go_ref, fw_send.at[i]).wait()
        return carry

    lax.fori_loop(1, N_DP // 2, wait_go_sent, 0)
    pltpu.make_async_copy(go_ref, go_ref, fw_send.at[0]).wait()
    for step in range(1, 5):
        for chunk in range(CHUNKS):
            for way in (1, -1):
                if has(step, chunk, way):
                    ring(step, chunk, way).wait_send()
    for store in stores:
        store.wait()

    wait_box(finbox, f_recv)
    for c in range(2):
        update_ref[:, c * 128 : (c + 1) * 128] = finbox[:, c].reshape(256, 128)
    wait_sent(fbox, f_send)


def tables(owners):
    owner_of = owners.reshape(-1)
    ids = jnp.arange(owner_of.shape[0], dtype=jnp.int32)
    earlier = (owner_of[:, None] == owner_of[None, :]) & (ids[None, :] < ids[:, None])
    pos = owner_of * 2 + jnp.sum(earlier.astype(jnp.int32), axis=1)
    places = jnp.arange(2 * N_DP, dtype=jnp.int32)
    hit = (pos[None, :] == places[:, None]).astype(jnp.int32)
    inv = jnp.sum(hit * (ids[None, :] + 1), axis=1) - 1
    return inv, pos


def on_device(acts, grad_out, owners, left_stats, right_stats):
    inv, pos = tables(owners)
    f32, bf16 = jnp.float32, jnp.bfloat16
    dma = pltpu.SemaphoreType.DMA
    vmem = pl.BlockSpec(memory_space=pltpu.VMEM)
    smem = pl.BlockSpec(memory_space=pltpu.SMEM)
    hbm = pl.BlockSpec(memory_space=pl.ANY)
    return pl.pallas_call(
        kernel,
        name="shampoo",
        out_shape=(
            jax.ShapeDtypeStruct(left_stats.shape, f32),
            jax.ShapeDtypeStruct(right_stats.shape, f32),
            jax.ShapeDtypeStruct((256, 256), f32),
        ),
        in_specs=[smem, smem, hbm, hbm, hbm, hbm],
        out_specs=(hbm, vmem, vmem),
        scratch_shapes=[
            pltpu.VMEM((128, 1024), bf16),
            pltpu.VMEM((N_DP, 32, 128), bf16),
            pltpu.VMEM((N_Z, N_DP, 32, 128), bf16),
            pltpu.VMEM((N_DP, 128, 256), bf16),
            pltpu.VMEM((2, 512, 512), f32),
            pltpu.VMEM((2, 128, 128), f32),
            pltpu.VMEM((2, 512, 512), f32),
            pltpu.VMEM((16, 2, 16, 128), f32),
            pltpu.VMEM((N_DP, 2, 16, 128), f32),
            pltpu.VMEM((N_DP, 2, 16, 128), f32),
            pltpu.VMEM((N_DP, 2, 2, 8, 128), f32),
            pltpu.VMEM((N_DP, 2, 2, 8, 128), f32),
            pltpu.VMEM((N_DP, 2, 8, 128), f32),
            pltpu.VMEM((N_DP, 2, 8, 128), f32),
            dma((4,)), dma((2,)),
            dma((N_DP,)), dma((N_DP,)),
            dma((N_DP // 2,)), dma((N_DP,)), dma((N_DP // 2,)),
            dma((4, CHUNKS)), dma((4, CHUNKS)), dma((4, CHUNKS)), dma((4, CHUNKS)),
            dma((N_DP,)), dma((N_DP,)),
            dma((N_DP,)), dma((N_DP,)),
            dma((N_DP,)), dma((N_DP,)),
        ],
        compiler_params=pltpu.CompilerParams(
            collective_id=0, has_side_effects=True, vmem_limit_bytes=48 << 20
        ),
    )(inv, pos, acts, grad_out, left_stats, right_stats)


def solution(mesh):
    in_specs = (
        P("dp", ("tensor", "pre")),
        P("dp", ("tensor", "pre")),
        P(None, ("tensor", "pre")),
        P("dp", None, None, ("tensor", "pre")),
        P("dp", None, None, ("tensor", "pre")),
    )
    out_specs = (
        P("dp", None, None, ("tensor", "pre")),
        P("dp", None, None, ("tensor", "pre")),
        P("dp", ("tensor", "pre")),
    )
    return jax.shard_map(
        on_device, mesh=mesh, in_specs=in_specs, out_specs=out_specs, check_vma=False
    )
```

time: 621 us -> 105 us (0.17); the launches traced: 612 us -> 104 us
  waiting for transfers between devices: 327 us -> 0 us
  blocking collectives: 117 us -> 0 us
  matrix products: 110 us -> 0 us
  Pallas kernels: 0 us -> 95.5 us
  local copies, waits for them, and re-layouts: 30.2 us -> 7.8 us
  between operations: 14.9 us -> 0.67 us
  starting transfers between devices: 7.5 us -> 0 us
    all_gather x1 -> x0, waiting for transfers between devices: 120 us -> none  [on_device(): lax.all_gather(acts, ('tensor', 'pre'), axis=1, tiled=True)]
    all_to_all x1 -> x0, blocking collectives: 117 us -> none  [on_device(): lax.all_to_all(return_box, 'dp', split_axis=0, concat_axis=0, tiled=True)]
    dot_general x29 -> x0, matrix products: 110 us -> none  [the longest x22 42.5 us: matmul_hi(): jnp.einsum('...ij,...jk->...ik', left, right, precision=lax.Precision.HIG...]
    all_to_all x1 -> x0, waiting for transfers between devices: 108 us -> none  [on_device(): lax.all_to_all(outbox, 'dp', split_axis=0, concat_axis=0, tiled=True)]
    reduce_scatter x1 -> x0, waiting for transfers between devices: 98.5 us -> none  [on_device(): lax.psum_scatter(partial_grads, 'dp', scatter_dimension=0, tiled=True)]
    pallas_call x0 -> x1, Pallas kernels: none -> 95.5 us  [on_device(): pl.pallas_call(kernel, name='shampoo', out_shape=(jax.ShapeDtypeStruct(le...]
    reshape x2 -> x1, local copies, waits for them, and re-layouts: 20 us -> 0.09 us  [tables(): owner_of = owners.reshape(-1)]
    dot_general x2 -> x0, local copies, waits for them, and re-layouts: 8.27 us -> none  [the longest x1 8.24 us: on_device(): jnp.einsum('kos,kph->osph', weight, pieces, precision=lax.Precision.HIGHEST)]
  transfers between devices with their start and end apart: 3 -> 0, of which waited for: 3 -> 0; matrix products, arithmetic and copies ran while one was open for 0% -> 0% of each run, Pallas kernels for 0% -> 0%
where the time goes in v1:
time: 105 us; the launch traced here: 104 us
  Pallas kernels  95.5 us (91%)
  local copies, waits for them, and re-layouts  7.8 us (7%)
    pallas_call x1, Pallas kernels, on_device(): pl.pallas_call(kernel, name='shampoo', out_shape=(jax.ShapeDtypeStruct(le...  95.5 us
    unnamed x12, local copies, waits for them, and re-layouts  7.71 us

profile of v1, /device:TPU:1, one launch (start us, length us, event | category | flops | bytes accessed | tf_op | source)
XLA Modules:
  0.0 104.3 jit_solution(2926674733158894476)
XLA Ops:
  0.6 0.8 copy.10
  1.4 0.1 reshape.24
  1.5 0.2 convert_reduce_fusion
  1.7 0.1 select_reduce_fusion
  1.8 0.0 copy-start
  1.8 1.6 %copy-done = f32[1,2,512,512]{3,2,1,0:T(8,128)S(1)} copy-done((f32[1,2,512,512]{3,2,1,0:T(8,128)S(1)}, f32[1,2,512,512]{3,2,1,0:T(8,128)}, u32[]{:S(2)}) %copy-start) | copy-done | bytes 2097176
  3.4 0.0 copy-start.1
  3.4 0.9 copy-done.1
  4.3 0.0 copy-start.2
  4.3 0.9 copy-done.2
  5.2 0.0 copy-start.3
  5.2 0.8 copy-done.3
  6.1 95.5 %shampoo.1 = (f32[1,2,512,512]{3,2,1,0:T(8,128)S(1)}, f32[1,2,128,128]{3,2,1,0:T(8,128)S(1)}, f32[256,256]{1,0:T(8,128)S(1)}) custom-call(s32[64]{0:T(128)S(1)} %broadcast_add_fusion.inv, s32[32]{0:T(128)S(1)} %get-tuple-element.4.pos, bf16[128,1024]{1,0:T(8,128)(2,1)S(1)} %copy-done.1, bf16[128,256]{1,0:T(8,128)(2,1)S(1)} %copy-done.3, ...), custom_call_target="tpu_custom_call" | custom-call | tf_op jit(solution)/shard_map/shampoo/pallas_call | solution.py:380
  101.6 1.3 %copy.14 = f32[1,2,512,512]{3,2,1,0:T(8,128)} copy(f32[1,2,512,512]{3,2,1,0:T(8,128)S(1)} %get-tuple-element.8) | data formatting | bytes 4194304
  102.9 0.7 copy.15
  103.6 0.7 copy.16
  (2 shorter events, 0.0 us)
Async XLA Ops:
  1.8 1.6 %copy-start = (f32[1,2,512,512]{3,2,1,0:T(8,128)S(1)}, f32[1,2,512,512]{3,2,1,0:T(8,128)}, u32[]{:S(2)}) copy-start(f32[1,2,512,512]{3,2,1,0:T(8,128)} %left_hbm.1) | copy-start | bytes 6291460
  3.4 0.9 copy-start.1
  4.3 0.9 copy-start.2
  5.2 0.8 copy-start.3

commit v2 on v1

v2 whole, which is shorter than its diff:
```python
import jax
import jax.numpy as jnp
from jax import lax
from jax.experimental import pallas as pl
from jax.experimental.pallas import tpu as pltpu
from jax.sharding import PartitionSpec as P

MESH = pl.DeviceIdType.MESH
N_DP = 32
HALF = 16
N_Z = 8
CHUNKS = 4
PER = N_DP // CHUNKS
decay_rate = 0.95
graft_eps = 1e-06


def split(x):
    hi = x.astype(jnp.bfloat16)
    lo = (x - hi.astype(jnp.float32)).astype(jnp.bfloat16)
    return hi, lo


def dot(a, b, dims):
    return lax.dot_general(a, b, (dims, ((), ())), preferred_element_type=jnp.float32)


def mul(a, b, dims=((1,), (0,))):
    return dot(a[0], b[0], dims) + (dot(a[0], b[1], dims) + dot(a[1], b[0], dims))


def eye_of(n):
    rows = lax.broadcasted_iota(jnp.int32, (n, n), 0)
    cols = lax.broadcasted_iota(jnp.int32, (n, n), 1)
    return jnp.where(rows == cols, 1.25, 0.0).astype(jnp.float32)


def total(x):
    return jnp.sum(jnp.sum(x, axis=0, keepdims=True), axis=1, keepdims=True)


def right_steps(right, z_r, out):
    eye = eye_of(128)

    def first():
        n = z_r * right
        out["n"] = split(n)
        out["f1"] = split(eye - 0.25 * n)
        out["s"] = split(mul(out["f1"], out["f1"]))

    def fourth():
        out["q"] = split(mul(out["s"], out["s"]))

    def second():
        n = mul(out["q"], out["n"])
        out["n"] = split(n)
        out["f2"] = split(eye - 0.25 * n)

    def both():
        out["f12"] = split(mul(out["f1"], out["f2"]))
        out["s"] = split(mul(out["f2"], out["f2"]))

    def third():
        out["f3"] = split(eye - 0.25 * mul(out["q"], out["n"]))

    def last():
        out["root"] = split(mul(out["f12"], out["f3"]))

    return [first, fourth, second, both, fourth, third, last]


def precondition(g, left, right):
    eye = eye_of(512)
    z_l = 2.5 * lax.rsqrt(total(left * left))
    z_r = 2.5 * lax.rsqrt(total(right * right))
    made = {}
    steps = right_steps(right, z_r, made)

    def step():
        if steps:
            steps.pop(0)()

    m = z_l * left
    ms = split(m)
    fs = split(eye - 0.25 * m)
    step()
    gt = g.T
    ss = split(mul(fs, fs))
    step()
    v1 = 1.25 * gt - 0.25 * mul(split(gt), ms)
    qs = split(mul(ss, ss))
    step()
    m2s = split(mul(qs, ms))
    step()
    v2 = 1.25 * v1 - 0.25 * mul(split(v1), m2s)
    step()
    w = mul(split(v2), m2s)
    step()
    for _ in range(4):
        w = 1.25 * w - 0.25 * mul(split(w), m2s)
        step()
    v3 = 1.25 * v2 - 0.25 * w
    shaped = mul(made["root"], split(v3)).T
    shaped = shaped * (jnp.sqrt(jnp.sqrt(z_l)) * jnp.sqrt(jnp.sqrt(z_r)))
    count = 1.0 / (512 * 128)
    grad_mean = total(g * g) * count
    shaped_mean = total(shaped * shaped) * count
    return shaped * jnp.sqrt(grad_mean / (shaped_mean + graft_eps))


def kernel(
    inv, pos, acts_hbm, go_hbm, left_hbm, right_hbm,
    nl_out, nr_out, finbox,
    acts_v, out_a, a_buf, go_buf, left_v, right_v, nl_v, nr_v, pieces, outbox, inbox,
    retbox, rinbox, fbox,
    in_sem, out_sem, a_send, a_recv, go_send, go_recv,
    zr_send, zr_recv, zl_send, zl_recv,
    d_send, d_recv, r_send, r_recv, f_send, f_recv,
):
    me = lax.axis_index("dp")
    tensor = lax.axis_index("tensor")
    pre = lax.axis_index("pre")
    z = pre * 4 + tensor
    odd = lax.rem(me, 2)
    partner = me + 1 - 2 * odd

    load_acts = pltpu.make_async_copy(acts_hbm, acts_v, in_sem.at[0])
    load_acts.start()
    load_go = pltpu.make_async_copy(go_hbm, go_buf.at[0, 0], in_sem.at[1])
    load_go.start()
    load_left = pltpu.make_async_copy(left_hbm.at[0], left_v, in_sem.at[2])
    load_left.start()
    load_right = pltpu.make_async_copy(right_hbm.at[0], right_v, in_sem.at[3])
    load_right.start()

    def z_dev(zz):
        zz = lax.rem(zz + N_Z, N_Z)
        return {"tensor": lax.rem(zz, 4), "pre": zz // 4}

    def slice_of(zz):
        zz = lax.rem(zz + N_Z, N_Z)
        return lax.rem(zz, 4) * 2 + zz // 4

    def wait_for(ref, sem):
        pltpu.make_async_copy(ref, ref, sem).wait()

    def to_plane(begin, make):
        def one(i, carry):
            make(i, lax.rem(me + i, N_DP)).start()
            return carry

        lax.fori_loop(begin, N_DP, one, 0)

    barrier = pltpu.get_barrier_semaphore()

    def greet(i, carry):
        pl.semaphore_signal(
            barrier, inc=1, device_id={"dp": lax.rem(me + i, N_DP)}, device_id_type=MESH
        )
        return carry

    lax.fori_loop(1, N_DP, greet, 0)
    for step in (1, -1):
        pl.semaphore_signal(barrier, inc=1, device_id=z_dev(z + step), device_id_type=MESH)

    load_acts.wait()
    for c in range(8):
        turned = acts_v[:, c * 128 : (c + 1) * 128].T
        for e in range(8):
            row = c * 128 + e * 16
            out_a[(row % 512) // 16, (row // 512) * 16 : (row // 512) * 16 + 16] = turned[
                e * 16 : e * 16 + 16
            ]
    mine = slice_of(z)
    pltpu.make_async_copy(out_a.at[me], a_buf.at[mine, 0], a_recv.at[0]).start()

    pl.semaphore_wait(barrier, N_DP + 1)

    to_plane(1, lambda i, peer: pltpu.make_async_remote_copy(
        src_ref=out_a.at[peer], dst_ref=a_buf.at[mine, i],
        send_sem=a_send.at[0], recv_sem=a_recv.at[i // PER],
        device_id={"dp": peer}, device_id_type=MESH,
    ))
    load_go.wait()

    def send_go(j, carry):
        pltpu.make_async_remote_copy(
            src_ref=go_buf.at[0, 0], dst_ref=go_buf.at[0, j],
            send_sem=go_send.at[0], recv_sem=go_recv.at[0],
            device_id={"dp": lax.rem(me + 2 * j, N_DP)}, device_id_type=MESH,
        ).start()
        return carry

    lax.fori_loop(1, HALF, send_go, 0)

    def ring(step, chunk, way):
        sems = (zr_send, zr_recv) if way == 1 else (zl_send, zl_recv)
        ref = a_buf.at[slice_of(z - way * (step - 1)), pl.ds(chunk * PER, PER)]
        return pltpu.make_async_remote_copy(
            src_ref=ref, dst_ref=ref,
            send_sem=sems[0].at[step - 1, chunk], recv_sem=sems[1].at[step - 1, chunk],
            device_id=z_dev(z + way), device_id_type=MESH,
        )

    def arrived(step, chunk, way):
        sems = zr_recv if way == 1 else zl_recv
        wait_for(a_buf.at[slice_of(z - way * step), pl.ds(chunk * PER, PER)], sems.at[step - 1, chunk])

    def has(step, chunk, way):
        return step < 4 or (chunk < CHUNKS // 2) == (way == 1)

    for step in range(1, 5):
        for chunk in range(CHUNKS):
            if step == 1:
                wait_for(a_buf.at[mine, pl.ds(chunk * PER, PER)], a_recv.at[chunk])
            for way in (1, -1):
                if step > 1:
                    arrived(step - 1, chunk, way)
                if has(step, chunk, way):
                    ring(step, chunk, way).start()
        if step == 3:
            wait_for(go_buf.at[0, pl.ds(1, HALF - 1)], go_recv.at[0])
            for src, dst in (
                (go_buf.at[0, pl.ds(odd, HALF - 1)], go_buf.at[1, pl.ds(0, HALF - 1)]),
                (go_buf.at[0, (HALF - 1) * (1 - odd)], go_buf.at[1, HALF - 1]),
            ):
                pltpu.make_async_remote_copy(
                    src_ref=src, dst_ref=dst, send_sem=go_send.at[1], recv_sem=go_recv.at[1],
                    device_id={"dp": partner}, device_id_type=MESH,
                ).start()

    wait_for(out_a.at[pl.ds(0, N_DP - 1)], a_send.at[0])
    wait_for(go_buf.at[0, pl.ds(1, HALF - 1)], go_send.at[0])
    wait_for(go_buf.at[1], go_recv.at[1])
    wait_for(go_buf.at[0], go_send.at[1])
    load_left.wait()
    load_right.wait()
    for chunk in range(CHUNKS):
        arrived(4, chunk, 1 if chunk < CHUNKS // 2 else -1)

    acc = jnp.zeros((256, 256), jnp.float32)
    for m in range(HALF):
        lhs = jnp.concatenate(
            [a_buf[:, 2 * m].reshape(256, 128), a_buf[:, 2 * m + 1].reshape(256, 128)], axis=1
        )
        rhs = jnp.concatenate([go_buf[0, m], go_buf[1, m]], axis=0)
        acc = acc + jnp.dot(lhs, rhs, preferred_element_type=jnp.float32)
    for c in range(2):
        pieces[:, c] = acc[:, c * 128 : (c + 1) * 128].reshape(16, 16, 128)

    for s in range(2):
        def fill(o):
            block = inv[2 * o + s]
            used = jnp.maximum(block, 0)
            value = pieces[used // 2, lax.rem(used, 2)]
            outbox[s, o] = jnp.where(block >= 0, value, 0.0)

        def to_owner(i, peer):
            fill(peer)
            return pltpu.make_async_remote_copy(
                src_ref=outbox.at[s, peer], dst_ref=inbox.at[s, me],
                send_sem=d_send.at[s], recv_sem=d_recv.at[s],
                device_id={"dp": peer}, device_id_type=MESH,
            )

        fill(me)
        pltpu.make_async_copy(outbox.at[s, me], inbox.at[s, me], d_recv.at[s]).start()
        to_plane(1, to_owner)

    for step in range(1, 5):
        for chunk in range(CHUNKS):
            for way in (1, -1):
                if has(step, chunk, way):
                    ring(step, chunk, way).wait_send()

    stores = []
    for s in range(2):
        wait_for(inbox.at[s], d_recv.at[s])
        g = inbox[s].reshape(512, 128)
        gs = split(g)
        nl_v[s] = decay_rate * left_v[s] + mul(gs, gs, ((1,), (1,)))
        nr_v[s] = decay_rate * right_v[s] + mul(gs, gs, ((0,), (0,)))
        for k, (src, dst) in enumerate(((nl_v.at[s], nl_out.at[0, s]), (nr_v.at[s], nr_out.at[0, s]))):
            store = pltpu.make_async_copy(src, dst, out_sem.at[2 * s + k])
            store.start()
            stores.append(store)
        shaped = precondition(g, nl_v[s], nr_v[s])
        for half in range(2):
            retbox[s, :, half] = shaped[half * 256 : (half + 1) * 256].reshape(N_DP, 8, 128)
        pltpu.make_async_copy(retbox.at[s, me], rinbox.at[s, me], r_recv.at[s]).start()
        to_plane(1, lambda i, peer: pltpu.make_async_remote_copy(
            src_ref=retbox.at[s, peer], dst_ref=rinbox.at[s, me],
            send_sem=r_send.at[s], recv_sem=r_recv.at[s],
            device_id={"dp": peer}, device_id_type=MESH,
        ))
    for s in range(2):
        wait_for(outbox.at[s, pl.ds(0, N_DP - 1)], d_send.at[s])
    for s in range(2):
        wait_for(rinbox.at[s], r_recv.at[s])

    def pick(d):
        for c in range(2):
            where = pos[c * 16 + d // 2]
            fbox[d, c] = rinbox[lax.rem(where, 2), where // 2, lax.rem(d, 2)]

    def to_holder(i, peer):
        pick(peer)
        return pltpu.make_async_remote_copy(
            src_ref=fbox.at[peer], dst_ref=finbox.at[me],
            send_sem=f_send.at[0], recv_sem=f_recv.at[0],
            device_id={"dp": peer}, device_id_type=MESH,
        )

    pick(me)
    pltpu.make_async_copy(fbox.at[me], finbox.at[me], f_recv.at[0]).start()
    to_plane(1, to_holder)

    for s in range(2):
        wait_for(retbox.at[s, pl.ds(0, N_DP - 1)], r_send.at[s])
    for store in stores:
        store.wait()
    wait_for(fbox.at[pl.ds(0, N_DP - 1)], f_send.at[0])
    wait_for(finbox, f_recv.at[0])


def export(nl, nr, box, nl_hbm, nr_hbm, up_hbm, sem):
    pairs = [
        (nl.at[0, 0], nl_hbm.at[0, 0]),
        (nl.at[0, 1], nl_hbm.at[0, 1]),
        (nr, nr_hbm),
        (box.at[:, 0], up_hbm.at[:, :, pl.ds(0, 128)]),
        (box.at[:, 1], up_hbm.at[:, :, pl.ds(128, 128)]),
    ]
    copies = [pltpu.make_async_copy(src, dst, sem.at[i]) for i, (src, dst) in enumerate(pairs)]
    for copy in copies:
        copy.start()
    for copy in copies:
        copy.wait()


def tables(owners):
    owner_of = owners.T.reshape(-1)
    at = jnp.arange(2 * 16, dtype=jnp.int32)
    ids = (at % 16) * 2 + at // 16
    earlier = (owner_of[:, None] == owner_of[None, :]) & (ids[None, :] < ids[:, None])
    pos = owner_of * 2 + jnp.sum(earlier.astype(jnp.int32), axis=1)
    places = jnp.arange(2 * N_DP, dtype=jnp.int32)
    hit = (pos[None, :] == places[:, None]).astype(jnp.int32)
    inv = jnp.sum(hit * (ids[None, :] + 1), axis=1) - 1
    return inv, pos


def on_device(acts, grad_out, owners, left_stats, right_stats):
    inv, pos = tables(owners)
    f32, bf16 = jnp.float32, jnp.bfloat16
    dma = pltpu.SemaphoreType.DMA
    vmem = pl.BlockSpec(memory_space=pltpu.VMEM)
    smem = pl.BlockSpec(memory_space=pltpu.SMEM)
    hbm = pl.BlockSpec(memory_space=pl.ANY)
    far = pl.BlockSpec(memory_space=pltpu.HBM)
    left_out = jax.ShapeDtypeStruct(left_stats.shape, f32)
    right_out = jax.ShapeDtypeStruct(right_stats.shape, f32)
    box = jax.ShapeDtypeStruct((N_DP, 2, 8, 128), f32)
    rows = jax.ShapeDtypeStruct((N_DP, 8, 256), f32)
    results = pl.pallas_call(
        kernel,
        name="shampoo",
        out_shape=(left_out, right_out, box),
        in_specs=[smem, smem, far, far, far, far],
        out_specs=(hbm, hbm, hbm),
        scratch_shapes=[
            pltpu.VMEM((128, 1024), bf16),
            pltpu.VMEM((N_DP, 32, 128), bf16),
            pltpu.VMEM((N_Z, N_DP, 32, 128), bf16),
            pltpu.VMEM((2, HALF, 128, 256), bf16),
            pltpu.VMEM((2, 512, 512), f32),
            pltpu.VMEM((2, 128, 128), f32),
            pltpu.VMEM((2, 512, 512), f32),
            pltpu.VMEM((2, 128, 128), f32),
            pltpu.VMEM((16, 2, 16, 128), f32),
            pltpu.VMEM((2, N_DP, 16, 128), f32),
            pltpu.VMEM((2, N_DP, 16, 128), f32),
            pltpu.VMEM((2, N_DP, 2, 8, 128), f32),
            pltpu.VMEM((2, N_DP, 2, 8, 128), f32),
            pltpu.VMEM((N_DP, 2, 8, 128), f32),
            dma((4,)), dma((4,)),
            dma((1,)), dma((CHUNKS,)),
            dma((2,)), dma((2,)),
            dma((4, CHUNKS)), dma((4, CHUNKS)), dma((4, CHUNKS)), dma((4, CHUNKS)),
            dma((2,)), dma((2,)),
            dma((2,)), dma((2,)),
            dma((1,)), dma((1,)),
        ],
        compiler_params=pltpu.CompilerParams(
            collective_id=0, has_side_effects=True, vmem_limit_bytes=32 << 20
        ),
    )(inv, pos, *(pltpu.with_memory_space_constraint(x, pltpu.HBM) for x in (
        acts, grad_out, left_stats, right_stats
    )))
    new_left, new_right, update = pl.pallas_call(
        export,
        name="export",
        out_shape=(left_out, right_out, rows),
        in_specs=[hbm, hbm, hbm],
        out_specs=(far, far, far),
        scratch_shapes=[dma((5,))],
        compiler_params=pltpu.CompilerParams(vmem_limit_bytes=16 << 20),
    )(*results)
    return new_left, new_right, update.reshape(256, 256)


def solution(mesh):
    in_specs = (
        P("dp", ("tensor", "pre")),
        P("dp", ("tensor", "pre")),
        P(None, ("tensor", "pre")),
        P("dp", None, None, ("tensor", "pre")),
        P("dp", None, None, ("tensor", "pre")),
    )
    out_specs = (
        P("dp", None, None, ("tensor", "pre")),
        P("dp", None, None, ("tensor", "pre")),
        P("dp", ("tensor", "pre")),
    )
    return jax.shard_map(
        on_device, mesh=mesh, in_specs=in_specs, out_specs=out_specs, check_vma=False
    )
```

time: 105 us -> 86.9 us (0.83)
  Pallas kernels: 95.5 us -> 85 us
  local copies, waits for them, and re-layouts: 7.8 us -> 0.76 us
    pallas_call x1 -> x2, Pallas kernels: 95.5 us -> 85 us  [the longest x1 83.6 us: on_device(): pl.pallas_call(kernel, name='shampoo', out_shape=(left_out, right_out, bo...]
    unnamed x12 -> x0, local copies, waits for them, and re-layouts: 7.71 us -> none
where the time goes in v2:
time: 86.9 us; the launch traced here: 86.7 us
  Pallas kernels  85 us (98%)
    pallas_call x1, Pallas kernels, on_device(): pl.pallas_call(kernel, name='shampoo', out_shape=(left_out, right_out, bo...  83.6 us

profile of v2, /device:TPU:1, one launch (start us, length us, event | category | flops | bytes accessed | tf_op | source)
XLA Modules:
  0.0 86.7 jit_solution(17273738736388503484)
XLA Ops:
  0.6 0.8 reshape.70
  1.4 0.2 convert_reduce_fusion
  1.6 0.1 select_reduce_fusion
  1.7 83.6 %shampoo.1 = (f32[1,2,512,512]{3,2,1,0:T(8,128)S(1)}, f32[1,2,128,128]{3,2,1,0:T(8,128)S(1)}, f32[32,2,8,128]{3,2,1,0:T(8,128)S(1)}) custom-call(s32[64]{0:T(128)S(1)} %broadcast_add_fusion.inv, s32[32]{0:T(128)S(1)} %get-tuple-element.15.pos, bf16[128,1024]{1,0:T(8,128)(2,1)} %acts_hbm.1, bf16[128,256]{1,0:T(8,128)(2,1)} %go_hbm.1, ...), custom_call_target="tpu_custom_call" | custom-call | tf_op jit(solution)/shard_map/shampoo/pallas_call | solution.py:365
  85.3 1.5 %export.1 = (f32[1,2,512,512]{3,2,1,0:T(8,128)}, f32[1,2,128,128]{3,2,1,0:T(8,128)}, f32[32,8,256]{2,1,0:T(8,128)}) custom-call(f32[1,2,512,512]{3,2,1,0:T(8,128)S(1)} %get-tuple-element.9.nl, f32[1,2,128,128]{3,2,1,0:T(8,128)S(1)} %get-tuple-element.10.nr, f32[32,2,8,128]{3,2,1,0:T(8,128)S(1)} %get-tuple-element.11.box), custom_call_target="tpu_custom_call" | custom-call | tf_op jit(solution)/shard_map/export/pallas_call | solution.py:400
  (3 shorter events, 0.0 us)

commit v3 on v2

--- a/solution.py
+++ b/solution.py
@@ -108,10 +108,29 @@
     return shaped * jnp.sqrt(grad_mean / (shaped_mean + graft_eps))
 
 
+def tables(owners):
+    shape = (N_DP, 128)
+    sub = lax.broadcasted_iota(jnp.int32, shape, 0)
+    lane = lax.broadcasted_iota(jnp.int32, shape, 1)
+    across = jnp.full(shape, -1, jnp.int32)
+    down = jnp.zeros(shape, jnp.int32)
+    for k in range(N_DP):
+        owner = owners[k % 2, k // 2]
+        across = jnp.where(lane == k, owner, across)
+        down = jnp.where(sub == k, owner, down)
+    same = across == down
+    place = 2 * across[:1] + jnp.sum(
+        jnp.where(same & (sub < lane), 1, 0), axis=0, keepdims=True
+    )
+    place_down = 2 * down + jnp.sum(jnp.where(same & (lane < sub), 1, 0), axis=1, keepdims=True)
+    block = jnp.sum(jnp.where(place_down == lane, sub + 1, 0), axis=0, keepdims=True) - 1
+    return block, place
+
+
 def kernel(
-    inv, pos, acts_hbm, go_hbm, left_hbm, right_hbm,
+    owners_hbm, acts_hbm, go_hbm, left_hbm, right_hbm,
     nl_out, nr_out, finbox,
-    acts_v, out_a, a_buf, go_buf, left_v, right_v, nl_v, nr_v, pieces, outbox, inbox,
+    owners_s, table_v, table_s, acts_v, out_a, a_buf, go_buf, left_v, right_v, nl_v, nr_v, pieces, outbox, inbox,
     retbox, rinbox, fbox,
     in_sem, out_sem, a_send, a_recv, go_send, go_recv,
     zr_send, zr_recv, zl_send, zl_recv,
@@ -123,10 +142,14 @@
     z = pre * 4 + tensor
     odd = lax.rem(me, 2)
     partner = me + 1 - 2 * odd
-
+    column = me // PER
+    own = lax.rem(me, PER) // 2
+
+    load_owners = pltpu.make_async_copy(owners_hbm, owners_s, in_sem.at[4])
+    load_owners.start()
     load_acts = pltpu.make_async_copy(acts_hbm, acts_v, in_sem.at[0])
     load_acts.start()
-    load_go = pltpu.make_async_copy(go_hbm, go_buf.at[0, 0], in_sem.at[1])
+    load_go = pltpu.make_async_copy(go_hbm, go_buf.at[odd, own], in_sem.at[1])
     load_go.start()
     load_left = pltpu.make_async_copy(left_hbm.at[0], left_v, in_sem.at[2])
     load_left.start()
@@ -163,35 +186,41 @@
     for step in (1, -1):
         pl.semaphore_signal(barrier, inc=1, device_id=z_dev(z + step), device_id_type=MESH)
 
+    mine = slice_of(z)
     load_acts.wait()
-    for c in range(8):
-        turned = acts_v[:, c * 128 : (c + 1) * 128].T
-        for e in range(8):
-            row = c * 128 + e * 16
-            out_a[(row % 512) // 16, (row // 512) * 16 : (row // 512) * 16 + 16] = turned[
-                e * 16 : e * 16 + 16
-            ]
-    mine = slice_of(z)
-    pltpu.make_async_copy(out_a.at[me], a_buf.at[mine, 0], a_recv.at[0]).start()
-
-    pl.semaphore_wait(barrier, N_DP + 1)
-
-    to_plane(1, lambda i, peer: pltpu.make_async_remote_copy(
-        src_ref=out_a.at[peer], dst_ref=a_buf.at[mine, i],
-        send_sem=a_send.at[0], recv_sem=a_recv.at[i // PER],
-        device_id={"dp": peer}, device_id_type=MESH,
-    ))
+    for hop in range(CHUNKS):
+        goal = lax.rem(column + hop, CHUNKS)
+        for part in range(2):
+            start = pl.multiple_of((goal + part * CHUNKS) * 128, 128)
+            turned = acts_v[:, pl.ds(start, 128)].T
+            for e in range(PER):
+                out_a[goal * PER + e, part * 16 : part * 16 + 16] = turned[e * 16 : e * 16 + 16]
+        if hop == 0:
+            pltpu.make_async_copy(
+                out_a.at[me], a_buf.at[mine, lax.rem(me, PER)], a_recv.at[0]
+            ).start()
+            pl.semaphore_wait(barrier, N_DP + 1)
+
+        def send_a(i, carry):
+            peer = goal * PER + lax.rem(me + i, PER)
+            pltpu.make_async_remote_copy(
+                src_ref=out_a.at[peer], dst_ref=a_buf.at[mine, hop * PER + lax.rem(me, PER)],
+                send_sem=a_send.at[0], recv_sem=a_recv.at[hop],
+                device_id={"dp": peer}, device_id_type=MESH,
+            ).start()
+            return carry
+
+        lax.fori_loop(1 if hop == 0 else 0, PER, send_a, 0)
     load_go.wait()
 
-    def send_go(j, carry):
+    def send_go(j):
+        hop, turn = j // 4, j % 4
+        peer = lax.rem(column + hop, CHUNKS) * PER + lax.rem(me + 2 * turn, PER)
         pltpu.make_async_remote_copy(
-            src_ref=go_buf.at[0, 0], dst_ref=go_buf.at[0, j],
+            src_ref=go_buf.at[odd, own], dst_ref=go_buf.at[odd, hop * 4 + own],
             send_sem=go_send.at[0], recv_sem=go_recv.at[0],
-            device_id={"dp": lax.rem(me + 2 * j, N_DP)}, device_id_type=MESH,
+            device_id={"dp": peer}, device_id_type=MESH,
         ).start()
-        return carry
-
-    lax.fori_loop(1, HALF, send_go, 0)
 
     def ring(step, chunk, way):
         sems = (zr_send, zr_recv) if way == 1 else (zl_send, zl_recv)
@@ -209,6 +238,7 @@
     def has(step, chunk, way):
         return step < 4 or (chunk < CHUNKS // 2) == (way == 1)
 
+    waiting = list(range(1, HALF))
     for step in range(1, 5):
         for chunk in range(CHUNKS):
             if step == 1:
@@ -218,21 +248,27 @@
                     arrived(step - 1, chunk, way)
                 if has(step, chunk, way):
                     ring(step, chunk, way).start()
-        if step == 3:
-            wait_for(go_buf.at[0, pl.ds(1, HALF - 1)], go_recv.at[0])
-            for src, dst in (
-                (go_buf.at[0, pl.ds(odd, HALF - 1)], go_buf.at[1, pl.ds(0, HALF - 1)]),
-                (go_buf.at[0, (HALF - 1) * (1 - odd)], go_buf.at[1, HALF - 1]),
-            ):
-                pltpu.make_async_remote_copy(
-                    src_ref=src, dst_ref=dst, send_sem=go_send.at[1], recv_sem=go_recv.at[1],
-                    device_id={"dp": partner}, device_id_type=MESH,
-                ).start()
-
+            for _ in range(2):
+                if waiting:
+                    send_go(waiting.pop(0))
+
+    load_owners.wait()
+    block, place = tables(owners_s)
+    table_v[0:1] = block
+    table_v[1:2] = place
+    load_table = pltpu.make_async_copy(table_v, table_s, in_sem.at[5])
+    load_table.start()
+
+    wait_for(go_buf.at[0, pl.ds(1, HALF - 1)], go_recv.at[0])
+    pltpu.make_async_remote_copy(
+        src_ref=go_buf.at[odd], dst_ref=go_buf.at[odd], send_sem=go_send.at[1], recv_sem=go_recv.at[1],
+        device_id={"dp": partner}, device_id_type=MESH,
+    ).start()
     wait_for(out_a.at[pl.ds(0, N_DP - 1)], a_send.at[0])
     wait_for(go_buf.at[0, pl.ds(1, HALF - 1)], go_send.at[0])
     wait_for(go_buf.at[1], go_recv.at[1])
     wait_for(go_buf.at[0], go_send.at[1])
+    load_table.wait()
     load_left.wait()
     load_right.wait()
     for chunk in range(CHUNKS):
@@ -250,7 +286,7 @@
 
     for s in range(2):
         def fill(o):
-            block = inv[2 * o + s]
+            block = table_s[0, 2 * o + s]
             used = jnp.maximum(block, 0)
             value = pieces[used // 2, lax.rem(used, 2)]
             outbox[s, o] = jnp.where(block >= 0, value, 0.0)
@@ -300,7 +336,7 @@
 
     def pick(d):
         for c in range(2):
-            where = pos[c * 16 + d // 2]
+            where = table_s[1, 2 * (d // 2) + c]
             fbox[d, c] = rinbox[lax.rem(where, 2), where // 2, lax.rem(d, 2)]
 
     def to_holder(i, peer):
@@ -338,24 +374,10 @@
         copy.wait()
 
 
-def tables(owners):
-    owner_of = owners.T.reshape(-1)
-    at = jnp.arange(2 * 16, dtype=jnp.int32)
-    ids = (at % 16) * 2 + at // 16
-    earlier = (owner_of[:, None] == owner_of[None, :]) & (ids[None, :] < ids[:, None])
-    pos = owner_of * 2 + jnp.sum(earlier.astype(jnp.int32), axis=1)
-    places = jnp.arange(2 * N_DP, dtype=jnp.int32)
-    hit = (pos[None, :] == places[:, None]).astype(jnp.int32)
-    inv = jnp.sum(hit * (ids[None, :] + 1), axis=1) - 1
-    return inv, pos
-
-
 def on_device(acts, grad_out, owners, left_stats, right_stats):
-    inv, pos = tables(owners)
     f32, bf16 = jnp.float32, jnp.bfloat16
     dma = pltpu.SemaphoreType.DMA
     vmem = pl.BlockSpec(memory_space=pltpu.VMEM)
-    smem = pl.BlockSpec(memory_space=pltpu.SMEM)
     hbm = pl.BlockSpec(memory_space=pl.ANY)
     far = pl.BlockSpec(memory_space=pltpu.HBM)
     left_out = jax.ShapeDtypeStruct(left_stats.shape, f32)
@@ -366,9 +388,12 @@
         kernel,
         name="shampoo",
         out_shape=(left_out, right_out, box),
-        in_specs=[smem, smem, far, far, far, far],
+        in_specs=[far, far, far, far, far],
         out_specs=(hbm, hbm, hbm),
         scratch_shapes=[
+            pltpu.SMEM((2, 16), jnp.int32),
+            pltpu.VMEM((8, 128), jnp.int32),
+            pltpu.SMEM((8, 128), jnp.int32),
             pltpu.VMEM((128, 1024), bf16),
             pltpu.VMEM((N_DP, 32, 128), bf16),
             pltpu.VMEM((N_Z, N_DP, 32, 128), bf16),
@@ -383,7 +408,7 @@
             pltpu.VMEM((2, N_DP, 2, 8, 128), f32),
             pltpu.VMEM((2, N_DP, 2, 8, 128), f32),
             pltpu.VMEM((N_DP, 2, 8, 128), f32),
-            dma((4,)), dma((4,)),
+            dma((6,)), dma((4,)),
             dma((1,)), dma((CHUNKS,)),
             dma((2,)), dma((2,)),
             dma((4, CHUNKS)), dma((4, CHUNKS)), dma((4, CHUNKS)), dma((4, CHUNKS)),
@@ -394,8 +419,8 @@
         compiler_params=pltpu.CompilerParams(
             collective_id=0, has_side_effects=True, vmem_limit_bytes=32 << 20
         ),
-    )(inv, pos, *(pltpu.with_memory_space_constraint(x, pltpu.HBM) for x in (
-        acts, grad_out, left_stats, right_stats
+    )(*(pltpu.with_memory_space_constraint(x, pltpu.HBM) for x in (
+        owners.T, acts, grad_out, left_stats, right_stats
     )))
     new_left, new_right, update = pl.pallas_call(
         export,

time: 86.9 us -> 78.7 us (0.906)
  Pallas kernels: 85 us -> 78 us
    pallas_call x1, Pallas kernels: 83.6 us -> 76.5 us  [on_device(): pl.pallas_call(kernel, name='shampoo', out_shape=(left_out, right_out, bo...]
where the time goes in v3:
time: 78.7 us; the launch traced here: 78.6 us
  Pallas kernels  78 us (99%)
    pallas_call x1, Pallas kernels, on_device(): pl.pallas_call(kernel, name='shampoo', out_shape=(left_out, right_out, bo...  76.5 us

profile of v3, /device:TPU:1, one launch (start us, length us, event | category | flops | bytes accessed | tf_op | source)
XLA Modules:
  0.0 78.6 jit_solution(18347826103406483786)
XLA Ops:
  0.6 76.5 %shampoo.1 = (f32[1,2,512,512]{3,2,1,0:T(8,128)S(1)}, f32[1,2,128,128]{3,2,1,0:T(8,128)S(1)}, f32[32,2,8,128]{3,2,1,0:T(8,128)S(1)}) custom-call(s32[2,16]{1,0:T(2,128)} %bitcast.2, bf16[128,1024]{1,0:T(8,128)(2,1)} %acts_hbm.1, bf16[128,256]{1,0:T(8,128)(2,1)} %go_hbm.1, f32[1,2,512,512]{3,2,1,0:T(8,128)} %left_hbm.1, f32[1,2,128,128]{3,2,1,0:T(8,128)} %right_hbm.1), custom_call_target="tpu_custom_call" | custom-call | tf_op jit(solution)/shard_map/shampoo/pallas_call | solution.py:387
  77.2 1.5 %export.1 = (f32[1,2,512,512]{3,2,1,0:T(8,128)}, f32[1,2,128,128]{3,2,1,0:T(8,128)}, f32[32,8,256]{2,1,0:T(8,128)}) custom-call(f32[1,2,512,512]{3,2,1,0:T(8,128)S(1)} %get-tuple-element.9.nl, f32[1,2,128,128]{3,2,1,0:T(8,128)S(1)} %get-tuple-element.10.nr, f32[32,2,8,128]{3,2,1,0:T(8,128)S(1)} %get-tuple-element.11.box), custom_call_target="tpu_custom_call" | custom-call | tf_op jit(solution)/shard_map/export/pallas_call | solution.py:425

commit v4 on v3

--- a/solution.py
+++ b/solution.py
@@ -11,6 +11,7 @@
 N_Z = 8
 CHUNKS = 4
 PER = N_DP // CHUNKS
+GO_PACE = (0, 3, 3, 0)
 decay_rate = 0.95
 graft_eps = 1e-06
 
@@ -129,12 +130,12 @@
 
 def kernel(
     owners_hbm, acts_hbm, go_hbm, left_hbm, right_hbm,
-    nl_out, nr_out, finbox,
-    owners_s, table_v, table_s, acts_v, out_a, a_buf, go_buf, left_v, right_v, nl_v, nr_v, pieces, outbox, inbox,
-    retbox, rinbox, fbox,
-    in_sem, out_sem, a_send, a_recv, go_send, go_recv,
+    nl_out, nr_out, up_box,
+    owners_s, table_v, table_s, acts_v, out_a, a_buf, go_buf, left_v, right_v,
+    sq, sf, rq, rf, tq, tf, uq, uf, old_left, old_right, pieces, gbox, outbox, inbox, half_v,
+    in_sem, a_send, a_recv, go_send, go_recv,
     zr_send, zr_recv, zl_send, zl_recv,
-    d_send, d_recv, r_send, r_recv, f_send, f_recv,
+    p_send, p_recv, g_send, g_recv, d_send, d_recv, x_send, x_recv,
 ):
     me = lax.axis_index("dp")
     tensor = lax.axis_index("tensor")
@@ -149,12 +150,12 @@
     load_owners.start()
     load_acts = pltpu.make_async_copy(acts_hbm, acts_v, in_sem.at[0])
     load_acts.start()
-    load_go = pltpu.make_async_copy(go_hbm, go_buf.at[odd, own], in_sem.at[1])
-    load_go.start()
     load_left = pltpu.make_async_copy(left_hbm.at[0], left_v, in_sem.at[2])
     load_left.start()
     load_right = pltpu.make_async_copy(right_hbm.at[0], right_v, in_sem.at[3])
     load_right.start()
+    load_go = pltpu.make_async_copy(go_hbm, go_buf.at[odd, own], in_sem.at[1])
+    load_go.start()
 
     def z_dev(zz):
         zz = lax.rem(zz + N_Z, N_Z)
@@ -167,12 +168,24 @@
     def wait_for(ref, sem):
         pltpu.make_async_copy(ref, ref, sem).wait()
 
-    def to_plane(begin, make):
+    def to_plane(begin, end, make):
         def one(i, carry):
-            make(i, lax.rem(me + i, N_DP)).start()
+            make(lax.rem(me + i, N_DP))
             return carry
 
-        lax.fori_loop(begin, N_DP, one, 0)
+        lax.fori_loop(max(begin, 1), end, one, 0)
+
+    def send(src, dst, sends, recvs, k, peer):
+        pltpu.make_async_remote_copy(
+            src_ref=src, dst_ref=dst, send_sem=sends.at[k], recv_sem=recvs.at[k],
+            device_id={"dp": peer}, device_id_type=MESH,
+        ).start()
+
+    def keep(src, dst, recvs, k):
+        pltpu.make_async_copy(src, dst, recvs.at[k]).start()
+
+    def wait_sent(box, sends, k):
+        wait_for(box.at[pl.ds(0, N_DP - 1)], sends.at[k])
 
     barrier = pltpu.get_barrier_semaphore()
 
@@ -211,16 +224,53 @@
             return carry
 
         lax.fori_loop(1 if hop == 0 else 0, PER, send_a, 0)
+
+    load_left.wait()
+    load_right.wait()
+    for s in range(2):
+        top = jnp.max(left_v[s], axis=0, keepdims=True)
+        scale = 32767.0 / jnp.maximum(top, 1e-30)
+        for a in range(4):
+            for i in range(3):
+                b = (a + i) % 4
+                level = left_v[s, a * 128 : a * 128 + 128, b * 128 : b * 128 + 128]
+                level = jnp.round(level * scale[:, b * 128 : b * 128 + 128])
+                level = level.astype(jnp.int32).astype(jnp.int16)
+                sq[a * 8 : a * 8 + 8, s, i * 16 : i * 16 + 16] = level.reshape(8, 16, 128)
+        for j in range(N_DP):
+            a = j // 8
+            sf[j, s, 0:4] = right_v[s, 4 * j : 4 * j + 4]
+            sf[j, s, 4:8] = jnp.broadcast_to(top[:, a * 128 : a * 128 + 128], (4, 128))
+    keep(sq.at[me], rq.at[me], p_recv, 0)
+    keep(sf.at[me], rf.at[me], p_recv, 1)
+
+    load_owners.wait()
+    block, place = tables(owners_s)
+    table_v[0:1] = block
+    table_v[1:2] = place
+    load_table = pltpu.make_async_copy(table_v, table_s, in_sem.at[5])
+    load_table.start()
+
     load_go.wait()
 
     def send_go(j):
         hop, turn = j // 4, j % 4
         peer = lax.rem(column + hop, CHUNKS) * PER + lax.rem(me + 2 * turn, PER)
-        pltpu.make_async_remote_copy(
-            src_ref=go_buf.at[odd, own], dst_ref=go_buf.at[odd, hop * 4 + own],
-            send_sem=go_send.at[0], recv_sem=go_recv.at[0],
-            device_id={"dp": peer}, device_id_type=MESH,
-        ).start()
+        send(go_buf.at[odd, own], go_buf.at[odd, hop * 4 + own], go_send, go_recv, 0, peer)
+
+    def send_old(peer):
+        send(sq.at[peer], rq.at[me], p_send, p_recv, 0, peer)
+        send(sf.at[peer], rf.at[me], p_send, p_recv, 1, peer)
+
+    def take_share(k):
+        where = table_s[1, k]
+        tq[k] = rq[where // 2, lax.rem(where, 2)]
+        tf[k] = rf[where // 2, lax.rem(where, 2)]
+
+    def send_share(peer):
+        take_share(peer)
+        send(tq.at[peer], uq.at[me], p_send, p_recv, 2, peer)
+        send(tf.at[peer], uf.at[me], p_send, p_recv, 3, peer)
 
     def ring(step, chunk, way):
         sems = (zr_send, zr_recv) if way == 1 else (zl_send, zl_recv)
@@ -248,29 +298,27 @@
                     arrived(step - 1, chunk, way)
                 if has(step, chunk, way):
                     ring(step, chunk, way).start()
-            for _ in range(2):
+            if step == 1:
+                to_plane(chunk * PER, (chunk + 1) * PER, send_old)
+            for _ in range(GO_PACE[step - 1]):
                 if waiting:
                     send_go(waiting.pop(0))
-
-    load_owners.wait()
-    block, place = tables(owners_s)
-    table_v[0:1] = block
-    table_v[1:2] = place
-    load_table = pltpu.make_async_copy(table_v, table_s, in_sem.at[5])
-    load_table.start()
+            if step == 4:
+                if chunk == 0:
+                    load_table.wait()
+                    wait_for(rq, p_recv.at[0])
+                    wait_for(rf, p_recv.at[1])
+                    take_share(me)
+                    keep(tq.at[me], uq.at[me], p_recv, 2)
+                    keep(tf.at[me], uf.at[me], p_recv, 3)
+                to_plane(chunk * PER, (chunk + 1) * PER, send_share)
 
     wait_for(go_buf.at[0, pl.ds(1, HALF - 1)], go_recv.at[0])
-    pltpu.make_async_remote_copy(
-        src_ref=go_buf.at[odd], dst_ref=go_buf.at[odd], send_sem=go_send.at[1], recv_sem=go_recv.at[1],
-        device_id={"dp": partner}, device_id_type=MESH,
-    ).start()
-    wait_for(out_a.at[pl.ds(0, N_DP - 1)], a_send.at[0])
+    send(go_buf.at[odd], go_buf.at[odd], go_send, go_recv, 1, partner)
+    wait_sent(out_a, a_send, 0)
     wait_for(go_buf.at[0, pl.ds(1, HALF - 1)], go_send.at[0])
     wait_for(go_buf.at[1], go_recv.at[1])
     wait_for(go_buf.at[0], go_send.at[1])
-    load_table.wait()
-    load_left.wait()
-    load_right.wait()
     for chunk in range(CHUNKS):
         arrived(4, chunk, 1 if chunk < CHUNKS // 2 else -1)
 
@@ -284,79 +332,74 @@
     for c in range(2):
         pieces[:, c] = acc[:, c * 128 : (c + 1) * 128].reshape(16, 16, 128)
 
-    for s in range(2):
-        def fill(o):
-            block = table_s[0, 2 * o + s]
-            used = jnp.maximum(block, 0)
+    keep(pieces.at[me // 2, odd], gbox.at[me], g_recv, 0)
+    to_plane(1, N_DP, lambda peer: send(
+        pieces.at[peer // 2, lax.rem(peer, 2)], gbox.at[me], g_send, g_recv, 0, peer
+    ))
+
+    def fill(o):
+        for s in range(2):
+            index = table_s[0, 2 * o + s]
+            used = jnp.maximum(index, 0)
             value = pieces[used // 2, lax.rem(used, 2)]
-            outbox[s, o] = jnp.where(block >= 0, value, 0.0)
-
-        def to_owner(i, peer):
-            fill(peer)
-            return pltpu.make_async_remote_copy(
-                src_ref=outbox.at[s, peer], dst_ref=inbox.at[s, me],
-                send_sem=d_send.at[s], recv_sem=d_recv.at[s],
-                device_id={"dp": peer}, device_id_type=MESH,
-            )
-
-        fill(me)
-        pltpu.make_async_copy(outbox.at[s, me], inbox.at[s, me], d_recv.at[s]).start()
-        to_plane(1, to_owner)
-
+            outbox[o, s] = jnp.where(index >= 0, value, 0.0)
+
+    def to_owner(peer):
+        fill(peer)
+        send(outbox.at[peer], inbox.at[me], d_send, d_recv, 0, peer)
+
+    to_plane(1, N_DP, to_owner)
+    fill(me)
+    keep(outbox.at[me], inbox.at[me], d_recv, 0)
+
+    wait_for(uq, p_recv.at[2])
+    wait_for(uf, p_recv.at[3])
+    for a in range(4):
+        for i in range(3):
+            b = (a + i) % 4
+            level = uq[a * 8 : a * 8 + 8, i * 16 : i * 16 + 16].reshape(128, 128)
+            level = level.astype(jnp.int32).astype(jnp.float32)
+            level = level * (uf[b * 8, 4:5] * (decay_rate / 32767.0))
+            old_left[a * 128 : a * 128 + 128, b * 128 : b * 128 + 128] = level
+            if i == 1:
+                old_left[b * 128 : b * 128 + 128, a * 128 : a * 128 + 128] = level.T
+    for j in range(N_DP):
+        old_right[4 * j : 4 * j + 4] = decay_rate * uf[j, 0:4]
+    wait_sent(sq, p_send, 0)
+    wait_sent(sf, p_send, 1)
+    wait_sent(tq, p_send, 2)
+    wait_sent(tf, p_send, 3)
     for step in range(1, 5):
         for chunk in range(CHUNKS):
             for way in (1, -1):
                 if has(step, chunk, way):
                     ring(step, chunk, way).wait_send()
 
-    stores = []
+    wait_for(gbox, g_recv.at[0])
+    g = gbox[...].reshape(512, 128)
+    gs = split(g)
+    shaped = precondition(
+        g,
+        old_left[...] + mul(gs, gs, ((1,), (1,))),
+        old_right[...] + mul(gs, gs, ((0,), (0,))),
+    )
+    for half in range(2):
+        half_v[half] = shaped[half * 256 : (half + 1) * 256]
+    send(half_v.at[1 - odd], up_box.at[odd], x_send, x_recv, 0, partner)
+    keep(half_v.at[odd], up_box.at[odd], x_recv, 1)
+
+    wait_for(inbox, d_recv.at[0])
     for s in range(2):
-        wait_for(inbox.at[s], d_recv.at[s])
-        g = inbox[s].reshape(512, 128)
-        gs = split(g)
-        nl_v[s] = decay_rate * left_v[s] + mul(gs, gs, ((1,), (1,)))
-        nr_v[s] = decay_rate * right_v[s] + mul(gs, gs, ((0,), (0,)))
-        for k, (src, dst) in enumerate(((nl_v.at[s], nl_out.at[0, s]), (nr_v.at[s], nr_out.at[0, s]))):
-            store = pltpu.make_async_copy(src, dst, out_sem.at[2 * s + k])
-            store.start()
-            stores.append(store)
-        shaped = precondition(g, nl_v[s], nr_v[s])
-        for half in range(2):
-            retbox[s, :, half] = shaped[half * 256 : (half + 1) * 256].reshape(N_DP, 8, 128)
-        pltpu.make_async_copy(retbox.at[s, me], rinbox.at[s, me], r_recv.at[s]).start()
-        to_plane(1, lambda i, peer: pltpu.make_async_remote_copy(
-            src_ref=retbox.at[s, peer], dst_ref=rinbox.at[s, me],
-            send_sem=r_send.at[s], recv_sem=r_recv.at[s],
-            device_id={"dp": peer}, device_id_type=MESH,
-        ))
-    for s in range(2):
-        wait_for(outbox.at[s, pl.ds(0, N_DP - 1)], d_send.at[s])
-    for s in range(2):
-        wait_for(rinbox.at[s], r_recv.at[s])
-
-    def pick(d):
-        for c in range(2):
-            where = table_s[1, 2 * (d // 2) + c]
-            fbox[d, c] = rinbox[lax.rem(where, 2), where // 2, lax.rem(d, 2)]
-
-    def to_holder(i, peer):
-        pick(peer)
-        return pltpu.make_async_remote_copy(
-            src_ref=fbox.at[peer], dst_ref=finbox.at[me],
-            send_sem=f_send.at[0], recv_sem=f_recv.at[0],
-            device_id={"dp": peer}, device_id_type=MESH,
-        )
-
-    pick(me)
-    pltpu.make_async_copy(fbox.at[me], finbox.at[me], f_recv.at[0]).start()
-    to_plane(1, to_holder)
-
-    for s in range(2):
-        wait_for(retbox.at[s, pl.ds(0, N_DP - 1)], r_send.at[s])
-    for store in stores:
-        store.wait()
-    wait_for(fbox.at[pl.ds(0, N_DP - 1)], f_send.at[0])
-    wait_for(finbox, f_recv.at[0])
+        gs = split(inbox[:, s].reshape(512, 128))
+        nl_out[0, s] = decay_rate * left_v[s] + mul(gs, gs, ((1,), (1,)))
+        nr_out[0, s] = decay_rate * right_v[s] + mul(gs, gs, ((0,), (0,)))
+
+    wait_for(pieces.at[pl.ds(0, 15)], g_send.at[0])
+    wait_for(pieces.at[15, 0], g_send.at[0])
+    wait_sent(outbox, d_send, 0)
+    wait_for(half_v.at[0], x_send.at[0])
+    wait_for(up_box.at[0], x_recv.at[0])
+    wait_for(up_box.at[0], x_recv.at[1])
 
 
 def export(nl, nr, box, nl_hbm, nr_hbm, up_hbm, sem):
@@ -364,8 +407,8 @@
         (nl.at[0, 0], nl_hbm.at[0, 0]),
         (nl.at[0, 1], nl_hbm.at[0, 1]),
         (nr, nr_hbm),
-        (box.at[:, 0], up_hbm.at[:, :, pl.ds(0, 128)]),
-        (box.at[:, 1], up_hbm.at[:, :, pl.ds(128, 128)]),
+        (box.at[0], up_hbm.at[:, pl.ds(0, 128)]),
+        (box.at[1], up_hbm.at[:, pl.ds(128, 128)]),
     ]
     copies = [pltpu.make_async_copy(src, dst, sem.at[i]) for i, (src, dst) in enumerate(pairs)]
     for copy in copies:
@@ -375,46 +418,52 @@
 
 
 def on_device(acts, grad_out, owners, left_stats, right_stats):
-    f32, bf16 = jnp.float32, jnp.bfloat16
+    f32, bf16, i16, i32 = jnp.float32, jnp.bfloat16, jnp.int16, jnp.int32
     dma = pltpu.SemaphoreType.DMA
     vmem = pl.BlockSpec(memory_space=pltpu.VMEM)
     hbm = pl.BlockSpec(memory_space=pl.ANY)
     far = pl.BlockSpec(memory_space=pltpu.HBM)
     left_out = jax.ShapeDtypeStruct(left_stats.shape, f32)
     right_out = jax.ShapeDtypeStruct(right_stats.shape, f32)
-    box = jax.ShapeDtypeStruct((N_DP, 2, 8, 128), f32)
-    rows = jax.ShapeDtypeStruct((N_DP, 8, 256), f32)
     results = pl.pallas_call(
         kernel,
         name="shampoo",
-        out_shape=(left_out, right_out, box),
+        out_shape=(left_out, right_out, jax.ShapeDtypeStruct((2, 256, 128), f32)),
         in_specs=[far, far, far, far, far],
-        out_specs=(hbm, hbm, hbm),
+        out_specs=(vmem, vmem, hbm),
         scratch_shapes=[
-            pltpu.SMEM((2, 16), jnp.int32),
-            pltpu.VMEM((8, 128), jnp.int32),
-            pltpu.SMEM((8, 128), jnp.int32),
+            pltpu.SMEM((2, 16), i32),
+            pltpu.VMEM((8, 128), i32),
+            pltpu.SMEM((8, 128), i32),
             pltpu.VMEM((128, 1024), bf16),
             pltpu.VMEM((N_DP, 32, 128), bf16),
             pltpu.VMEM((N_Z, N_DP, 32, 128), bf16),
             pltpu.VMEM((2, HALF, 128, 256), bf16),
             pltpu.VMEM((2, 512, 512), f32),
             pltpu.VMEM((2, 128, 128), f32),
-            pltpu.VMEM((2, 512, 512), f32),
-            pltpu.VMEM((2, 128, 128), f32),
+            pltpu.VMEM((N_DP, 2, 48, 128), i16),
+            pltpu.VMEM((N_DP, 2, 8, 128), f32),
+            pltpu.VMEM((N_DP, 2, 48, 128), i16),
+            pltpu.VMEM((N_DP, 2, 8, 128), f32),
+            pltpu.VMEM((N_DP, 48, 128), i16),
+            pltpu.VMEM((N_DP, 8, 128), f32),
+            pltpu.VMEM((N_DP, 48, 128), i16),
+            pltpu.VMEM((N_DP, 8, 128), f32),
+            pltpu.VMEM((512, 512), f32),
+            pltpu.VMEM((128, 128), f32),
             pltpu.VMEM((16, 2, 16, 128), f32),
-            pltpu.VMEM((2, N_DP, 16, 128), f32),
-            pltpu.VMEM((2, N_DP, 16, 128), f32),
-            pltpu.VMEM((2, N_DP, 2, 8, 128), f32),
-            pltpu.VMEM((2, N_DP, 2, 8, 128), f32),
-            pltpu.VMEM((N_DP, 2, 8, 128), f32),
-            dma((6,)), dma((4,)),
+            pltpu.VMEM((N_DP, 16, 128), f32),
+            pltpu.VMEM((N_DP, 2, 16, 128), f32),
+            pltpu.VMEM((N_DP, 2, 16, 128), f32),
+            pltpu.VMEM((2, 256, 128), f32),
+            dma((6,)),
             dma((1,)), dma((CHUNKS,)),
             dma((2,)), dma((2,)),
             dma((4, CHUNKS)), dma((4, CHUNKS)), dma((4, CHUNKS)), dma((4, CHUNKS)),
-            dma((2,)), dma((2,)),
-            dma((2,)), dma((2,)),
+            dma((4,)), dma((4,)),
             dma((1,)), dma((1,)),
+            dma((1,)), dma((1,)),
+            dma((1,)), dma((2,)),
         ],
         compiler_params=pltpu.CompilerParams(
             collective_id=0, has_side_effects=True, vmem_limit_bytes=32 << 20
@@ -422,16 +471,15 @@
     )(*(pltpu.with_memory_space_constraint(x, pltpu.HBM) for x in (
         owners.T, acts, grad_out, left_stats, right_stats
     )))
-    new_left, new_right, update = pl.pallas_call(
+    return pl.pallas_call(
         export,
         name="export",
-        out_shape=(left_out, right_out, rows),
+        out_shape=(left_out, right_out, jax.ShapeDtypeStruct((256, 256), f32)),
         in_specs=[hbm, hbm, hbm],
         out_specs=(far, far, far),
         scratch_shapes=[dma((5,))],
         compiler_params=pltpu.CompilerParams(vmem_limit_bytes=16 << 20),
     )(*results)
-    return new_left, new_right, update.reshape(256, 256)
 
 
 def solution(mesh):

time: 78.7 us -> 66.9 us (0.85)
  Pallas kernels: 78 us -> 66 us
    pallas_call x2, Pallas kernels: 78 us -> 66 us  [the longest x1 64.5 us: on_device(): pl.pallas_call(kernel, name='shampoo', out_shape=(left_out, right_out, ja...]
where the time goes in v4:
time: 66.9 us; the launch traced here: 66.6 us
  Pallas kernels  66 us (99%)
    pallas_call x1, Pallas kernels, on_device(): pl.pallas_call(kernel, name='shampoo', out_shape=(left_out, right_out, ja...  64.5 us
    pallas_call x1, Pallas kernels, on_device(): pl.pallas_call(export, name='export', out_shape=(left_out, right_out, jax...  1.48 us

profile of v4, /device:TPU:1, one launch (start us, length us, event | category | flops | bytes accessed | tf_op | source)
XLA Modules:
  0.0 66.6 jit_solution(15596246830099087580)
XLA Ops:
  0.6 64.5 %shampoo.1 = (f32[1,2,512,512]{3,2,1,0:T(8,128)S(1)}, f32[1,2,128,128]{3,2,1,0:T(8,128)S(1)}, f32[2,256,128]{2,1,0:T(8,128)S(1)}) custom-call(s32[2,16]{1,0:T(2,128)} %bitcast.1, bf16[128,1024]{1,0:T(8,128)(2,1)} %acts_hbm.1, bf16[128,256]{1,0:T(8,128)(2,1)} %go_hbm.1, f32[1,2,512,512]{3,2,1,0:T(8,128)} %left_hbm.1, f32[1,2,128,128]{3,2,1,0:T(8,128)} %right_hbm.1), custom_call_target="tpu_custom_call" | custom-call | tf_op jit(solution)/shard_map/shampoo/pallas_call | solution.py:428
  65.2 1.5 %export.1 = (f32[1,2,512,512]{3,2,1,0:T(8,128)}, f32[1,2,128,128]{3,2,1,0:T(8,128)}, f32[256,256]{1,0:T(8,128)}) custom-call(f32[1,2,512,512]{3,2,1,0:T(8,128)S(1)} %get-tuple-element.6.nl, f32[1,2,128,128]{3,2,1,0:T(8,128)S(1)} %get-tuple-element.7.nr, f32[2,256,128]{2,1,0:T(8,128)S(1)} %get-tuple-element.8.box), custom_call_target="tpu_custom_call" | custom-call | tf_op jit(solution)/shard_map/export/pallas_call | solution.py:474

commit v5 on v4

--- a/solution.py
+++ b/solution.py
@@ -1,3 +1,5 @@
+import math
+
 import jax
 import jax.numpy as jnp
 from jax import lax
@@ -11,7 +13,7 @@
 N_Z = 8
 CHUNKS = 4
 PER = N_DP // CHUNKS
-GO_PACE = (0, 3, 3, 0)
+LEVELS = 32760.0
 decay_rate = 0.95
 graft_eps = 1e-06
 
@@ -128,11 +130,21 @@
     return block, place
 
 
+def scale_of(stats):
+    top = jnp.maximum(jnp.max(stats, axis=0, keepdims=True), 1e-30)
+    code = jnp.ceil(jnp.log(top) * (256.0 / math.log(2.0)))
+    return code.astype(jnp.int32), LEVELS * jnp.exp2(code * (-1.0 / 256.0))
+
+
+def unit_of(code):
+    return (decay_rate / LEVELS) * jnp.exp2(code.astype(jnp.float32) * (1.0 / 256.0))
+
+
 def kernel(
     owners_hbm, acts_hbm, go_hbm, left_hbm, right_hbm,
     nl_out, nr_out, up_box,
     owners_s, table_v, table_s, acts_v, out_a, a_buf, go_buf, left_v, right_v,
-    sq, sf, rq, rf, tq, tf, uq, uf, old_left, old_right, pieces, gbox, outbox, inbox, half_v,
+    sq, rq, tq, uq, old_left, old_right, pieces, gbox, outbox, inbox, half_v,
     in_sem, a_send, a_recv, go_send, go_recv,
     zr_send, zr_recv, zl_send, zl_recv,
     p_send, p_recv, g_send, g_recv, d_send, d_recv, x_send, x_recv,
@@ -154,7 +166,7 @@
     load_left.start()
     load_right = pltpu.make_async_copy(right_hbm.at[0], right_v, in_sem.at[3])
     load_right.start()
-    load_go = pltpu.make_async_copy(go_hbm, go_buf.at[odd, own], in_sem.at[1])
+    load_go = pltpu.make_async_copy(go_hbm, go_buf.at[odd, 0, own], in_sem.at[1])
     load_go.start()
 
     def z_dev(zz):
@@ -225,52 +237,44 @@
 
         lax.fori_loop(1 if hop == 0 else 0, PER, send_a, 0)
 
-    load_left.wait()
-    load_right.wait()
-    for s in range(2):
-        top = jnp.max(left_v[s], axis=0, keepdims=True)
-        scale = 32767.0 / jnp.maximum(top, 1e-30)
-        for a in range(4):
-            for i in range(3):
-                b = (a + i) % 4
-                level = left_v[s, a * 128 : a * 128 + 128, b * 128 : b * 128 + 128]
-                level = jnp.round(level * scale[:, b * 128 : b * 128 + 128])
-                level = level.astype(jnp.int32).astype(jnp.int16)
-                sq[a * 8 : a * 8 + 8, s, i * 16 : i * 16 + 16] = level.reshape(8, 16, 128)
-        for j in range(N_DP):
-            a = j // 8
-            sf[j, s, 0:4] = right_v[s, 4 * j : 4 * j + 4]
-            sf[j, s, 4:8] = jnp.broadcast_to(top[:, a * 128 : a * 128 + 128], (4, 128))
-    keep(sq.at[me], rq.at[me], p_recv, 0)
-    keep(sf.at[me], rf.at[me], p_recv, 1)
-
-    load_owners.wait()
-    block, place = tables(owners_s)
-    table_v[0:1] = block
-    table_v[1:2] = place
-    load_table = pltpu.make_async_copy(table_v, table_s, in_sem.at[5])
-    load_table.start()
-
-    load_go.wait()
-
-    def send_go(j):
-        hop, turn = j // 4, j % 4
-        peer = lax.rem(column + hop, CHUNKS) * PER + lax.rem(me + 2 * turn, PER)
-        send(go_buf.at[odd, own], go_buf.at[odd, hop * 4 + own], go_send, go_recv, 0, peer)
+    def x_peer(hop):
+        return lax.rem(column + hop, CHUNKS) * PER + lax.rem(me, PER)
+
+    def y_peer(hop):
+        return column * PER + lax.rem(me + 2 * hop, PER)
+
+    def first_stage(hop):
+        near = go_buf.at[odd, 0, own, pl.ds(0, 64)]
+        far = go_buf.at[odd, 0, own, pl.ds(64, 64)]
+        send(near, go_buf.at[odd, hop, own, pl.ds(0, 64)], go_send, go_recv, 0, x_peer(hop))
+        send(far, far, go_send, go_recv, 1, y_peer(hop))
+
+    def second_stage(hop):
+        near = go_buf.at[odd, :, own, pl.ds(0, 64)]
+        far = go_buf.at[odd, 0, :, pl.ds(64, 64)]
+        send(near, near, go_send, go_recv, 2, y_peer(hop))
+        send(far, go_buf.at[odd, hop, :, pl.ds(64, 64)], go_send, go_recv, 3, x_peer(hop))
+
+    def wait_first(sems):
+        for k in (0, 1):
+            wait_for(go_buf.at[0, 0, pl.ds(0, 3), pl.ds(0, 64)], sems.at[k])
+
+    def wait_second(sems):
+        for k in (2, 3):
+            wait_for(go_buf.at[0, pl.ds(0, 3), :, pl.ds(0, 64)], sems.at[k])
 
     def send_old(peer):
         send(sq.at[peer], rq.at[me], p_send, p_recv, 0, peer)
-        send(sf.at[peer], rf.at[me], p_send, p_recv, 1, peer)
 
     def take_share(k):
         where = table_s[1, k]
-        tq[k] = rq[where // 2, lax.rem(where, 2)]
-        tf[k] = rf[where // 2, lax.rem(where, 2)]
+        for i in range(3):
+            tq[k, i * 16 : i * 16 + 16] = rq[where // 2, lax.rem(where, 2) * 3 + i]
+        tq[k, 48:64] = rq[where // 2, 6]
 
     def send_share(peer):
         take_share(peer)
-        send(tq.at[peer], uq.at[me], p_send, p_recv, 2, peer)
-        send(tf.at[peer], uf.at[me], p_send, p_recv, 3, peer)
+        send(tq.at[peer], uq.at[me], p_send, p_recv, 1, peer)
 
     def ring(step, chunk, way):
         sems = (zr_send, zr_recv) if way == 1 else (zl_send, zl_recv)
@@ -288,7 +292,75 @@
     def has(step, chunk, way):
         return step < 4 or (chunk < CHUNKS // 2) == (way == 1)
 
-    waiting = list(range(1, HALF))
+    codes_l = []
+
+    def level_left(s):
+        if s == 0:
+            load_left.wait()
+        code, scale = scale_of(left_v[s])
+        codes_l.append(code)
+        for a in range(4):
+            for i in range(3):
+                b = (a + i) % 4
+                level = left_v[s, a * 128 : a * 128 + 128, b * 128 : b * 128 + 128]
+                level = jnp.round(level * scale[:, b * 128 : b * 128 + 128])
+                level = level.astype(jnp.int32).astype(jnp.int16)
+                sq[a * 8 : a * 8 + 8, s * 3 + i] = level.reshape(8, 16, 128)
+
+    def level_right():
+        load_right.wait()
+        row = lax.broadcasted_iota(jnp.int32, (8, 128), 0)
+        rights, codes_r = [], []
+        for s in range(2):
+            code, scale = scale_of(right_v[s])
+            codes_r.append(code)
+            rights.append(jnp.round(right_v[s] * scale).astype(jnp.int32))
+        for a in range(4):
+            codes = [c[:, a * 128 : a * 128 + 128] for c in codes_l] + codes_r
+            low = jnp.where(
+                row < 4,
+                jnp.where(row < 2, codes[0], codes[1]),
+                jnp.where(row < 6, codes[2], codes[3]),
+            )
+            for j in range(8 * a, 8 * a + 8):
+                high = jnp.concatenate([r[4 * j : 4 * j + 4] for r in rights], axis=0)
+                sq[j, 6] = jnp.concatenate([high, low], axis=0).astype(jnp.int16)
+        keep(sq.at[me], rq.at[me], p_recv, 0)
+
+    def make_tables():
+        load_owners.wait()
+        block, place = tables(owners_s)
+        table_v[0:1] = block
+        table_v[1:2] = place
+        load_table.start()
+
+    def old(part):
+        to_plane(part * PER, (part + 1) * PER, send_old)
+
+    def share(part):
+        if part == 0:
+            load_table.wait()
+            wait_for(rq, p_recv.at[0])
+            take_share(me)
+            keep(tq.at[me], uq.at[me], p_recv, 1)
+        to_plane(part * PER, (part + 1) * PER, send_share)
+
+    load_table = pltpu.make_async_copy(table_v, table_s, in_sem.at[5])
+    plan = {
+        (1, 0): [load_go.wait, lambda: first_stage(1), lambda: level_left(0)],
+        (1, 1): [lambda: first_stage(2), lambda: level_left(1)],
+        (1, 2): [lambda: first_stage(3), level_right],
+        (1, 3): [lambda: old(0), lambda: old(1)],
+        (2, 0): [lambda: old(2), make_tables],
+        (2, 1): [lambda: old(3)],
+        (2, 2): [lambda: wait_first(go_recv), lambda: second_stage(1)],
+        (2, 3): [lambda: second_stage(2)],
+        (3, 0): [lambda: second_stage(3)],
+        (4, 0): [lambda: share(0)],
+        (4, 1): [lambda: share(1)],
+        (4, 2): [lambda: share(2)],
+        (4, 3): [lambda: share(3)],
+    }
     for step in range(1, 5):
         for chunk in range(CHUNKS):
             if step == 1:
@@ -298,27 +370,16 @@
                     arrived(step - 1, chunk, way)
                 if has(step, chunk, way):
                     ring(step, chunk, way).start()
-            if step == 1:
-                to_plane(chunk * PER, (chunk + 1) * PER, send_old)
-            for _ in range(GO_PACE[step - 1]):
-                if waiting:
-                    send_go(waiting.pop(0))
-            if step == 4:
-                if chunk == 0:
-                    load_table.wait()
-                    wait_for(rq, p_recv.at[0])
-                    wait_for(rf, p_recv.at[1])
-                    take_share(me)
-                    keep(tq.at[me], uq.at[me], p_recv, 2)
-                    keep(tf.at[me], uf.at[me], p_recv, 3)
-                to_plane(chunk * PER, (chunk + 1) * PER, send_share)
-
-    wait_for(go_buf.at[0, pl.ds(1, HALF - 1)], go_recv.at[0])
-    send(go_buf.at[odd], go_buf.at[odd], go_send, go_recv, 1, partner)
+            for act in plan.get((step, chunk), ()):
+                act()
+
+    wait_second(go_recv)
+    send(go_buf.at[odd], go_buf.at[odd], go_send, go_recv, 4, partner)
     wait_sent(out_a, a_send, 0)
-    wait_for(go_buf.at[0, pl.ds(1, HALF - 1)], go_send.at[0])
-    wait_for(go_buf.at[1], go_recv.at[1])
-    wait_for(go_buf.at[0], go_send.at[1])
+    wait_first(go_send)
+    wait_second(go_send)
+    wait_for(go_buf.at[1], go_recv.at[4])
+    wait_for(go_buf.at[0], go_send.at[4])
     for chunk in range(CHUNKS):
         arrived(4, chunk, 1 if chunk < CHUNKS // 2 else -1)
 
@@ -327,7 +388,7 @@
         lhs = jnp.concatenate(
             [a_buf[:, 2 * m].reshape(256, 128), a_buf[:, 2 * m + 1].reshape(256, 128)], axis=1
         )
-        rhs = jnp.concatenate([go_buf[0, m], go_buf[1, m]], axis=0)
+        rhs = jnp.concatenate([go_buf[0, m // 4, m % 4], go_buf[1, m // 4, m % 4]], axis=0)
         acc = acc + jnp.dot(lhs, rhs, preferred_element_type=jnp.float32)
     for c in range(2):
         pieces[:, c] = acc[:, c * 128 : (c + 1) * 128].reshape(16, 16, 128)
@@ -352,23 +413,26 @@
     fill(me)
     keep(outbox.at[me], inbox.at[me], d_recv, 0)
 
-    wait_for(uq, p_recv.at[2])
-    wait_for(uf, p_recv.at[3])
+    wait_for(uq, p_recv.at[1])
+    second = lax.rem(table_s[1, me], 2) == 1
     for a in range(4):
         for i in range(3):
             b = (a + i) % 4
+            codes = uq[b * 8, 48:64].astype(jnp.int32)
+            unit = unit_of(jnp.where(second, codes[10:11], codes[8:9]))
             level = uq[a * 8 : a * 8 + 8, i * 16 : i * 16 + 16].reshape(128, 128)
-            level = level.astype(jnp.int32).astype(jnp.float32)
-            level = level * (uf[b * 8, 4:5] * (decay_rate / 32767.0))
+            level = level.astype(jnp.int32).astype(jnp.float32) * unit
             old_left[a * 128 : a * 128 + 128, b * 128 : b * 128 + 128] = level
             if i == 1:
                 old_left[b * 128 : b * 128 + 128, a * 128 : a * 128 + 128] = level.T
+    codes = uq[0, 48:64].astype(jnp.int32)
+    unit = unit_of(jnp.where(second, codes[14:15], codes[12:13]))
     for j in range(N_DP):
-        old_right[4 * j : 4 * j + 4] = decay_rate * uf[j, 0:4]
+        level = uq[j, 48:64].astype(jnp.int32)
+        level = jnp.where(second, level[4:8], level[0:4])
+        old_right[4 * j : 4 * j + 4] = level.astype(jnp.float32) * unit
     wait_sent(sq, p_send, 0)
-    wait_sent(sf, p_send, 1)
-    wait_sent(tq, p_send, 2)
-    wait_sent(tf, p_send, 3)
+    wait_sent(tq, p_send, 1)
     for step in range(1, 5):
         for chunk in range(CHUNKS):
             for way in (1, -1):
@@ -438,17 +502,13 @@
             pltpu.VMEM((128, 1024), bf16),
             pltpu.VMEM((N_DP, 32, 128), bf16),
             pltpu.VMEM((N_Z, N_DP, 32, 128), bf16),
-            pltpu.VMEM((2, HALF, 128, 256), bf16),
+            pltpu.VMEM((2, 4, 4, 128, 256), bf16),
             pltpu.VMEM((2, 512, 512), f32),
             pltpu.VMEM((2, 128, 128), f32),
-            pltpu.VMEM((N_DP, 2, 48, 128), i16),
-            pltpu.VMEM((N_DP, 2, 8, 128), f32),
-            pltpu.VMEM((N_DP, 2, 48, 128), i16),
-            pltpu.VMEM((N_DP, 2, 8, 128), f32),
-            pltpu.VMEM((N_DP, 48, 128), i16),
-            pltpu.VMEM((N_DP, 8, 128), f32),
-            pltpu.VMEM((N_DP, 48, 128), i16),
-            pltpu.VMEM((N_DP, 8, 128), f32),
+            pltpu.VMEM((N_DP, 7, 16, 128), i16),
+            pltpu.VMEM((N_DP, 7, 16, 128), i16),
+            pltpu.VMEM((N_DP, 64, 128), i16),
+            pltpu.VMEM((N_DP, 64, 128), i16),
             pltpu.VMEM((512, 512), f32),
             pltpu.VMEM((128, 128), f32),
             pltpu.VMEM((16, 2, 16, 128), f32),
@@ -458,9 +518,9 @@
             pltpu.VMEM((2, 256, 128), f32),
             dma((6,)),
             dma((1,)), dma((CHUNKS,)),
+            dma((5,)), dma((5,)),
+            dma((4, CHUNKS)), dma((4, CHUNKS)), dma((4, CHUNKS)), dma((4, CHUNKS)),
             dma((2,)), dma((2,)),
-            dma((4, CHUNKS)), dma((4, CHUNKS)), dma((4, CHUNKS)), dma((4, CHUNKS)),
-            dma((4,)), dma((4,)),
             dma((1,)), dma((1,)),
             dma((1,)), dma((1,)),
             dma((1,)), dma((2,)),

time: 66.9 us -> 61 us (0.912)
  Pallas kernels: 66 us -> 60.2 us
    pallas_call x1, Pallas kernels: 64.5 us -> 58.7 us  [on_device(): pl.pallas_call(kernel, name='shampoo', out_shape=(left_out, right_out, ja...]
where the time goes in v5:
time: 61 us; the launch traced here: 60.8 us
  Pallas kernels  60.2 us (99%)
  between operations  0.64 us (1%)
    pallas_call x1, Pallas kernels, on_device(): pl.pallas_call(kernel, name='shampoo', out_shape=(left_out, right_out, ja...  58.7 us
    pallas_call x1, Pallas kernels, on_device(): pl.pallas_call(export, name='export', out_shape=(left_out, right_out, jax...  1.48 us

profile of v5, /device:TPU:1, one launch (start us, length us, event | category | flops | bytes accessed | tf_op | source)
XLA Modules:
  0.0 60.8 jit_solution(13619500732313665582)
XLA Ops:
  0.6 58.7 %shampoo.1 = (f32[1,2,512,512]{3,2,1,0:T(8,128)S(1)}, f32[1,2,128,128]{3,2,1,0:T(8,128)S(1)}, f32[2,256,128]{2,1,0:T(8,128)S(1)}) custom-call(s32[2,16]{1,0:T(2,128)} %bitcast.1, bf16[128,1024]{1,0:T(8,128)(2,1)} %acts_hbm.1, bf16[128,256]{1,0:T(8,128)(2,1)} %go_hbm.1, f32[1,2,512,512]{3,2,1,0:T(8,128)} %left_hbm.1, f32[1,2,128,128]{3,2,1,0:T(8,128)} %right_hbm.1), custom_call_target="tpu_custom_call" | custom-call | tf_op jit(solution)/shard_map/shampoo/pallas_call | solution.py:492
  59.3 1.5 %export.1 = (f32[1,2,512,512]{3,2,1,0:T(8,128)}, f32[1,2,128,128]{3,2,1,0:T(8,128)}, f32[256,256]{1,0:T(8,128)}) custom-call(f32[1,2,512,512]{3,2,1,0:T(8,128)S(1)} %get-tuple-element.6.nl, f32[1,2,128,128]{3,2,1,0:T(8,128)S(1)} %get-tuple-element.7.nr, f32[2,256,128]{2,1,0:T(8,128)S(1)} %get-tuple-element.8.box), custom_call_target="tpu_custom_call" | custom-call | tf_op jit(solution)/shard_map/export/pallas_call | solution.py:534

commit v6 on v5

--- a/solution.py
+++ b/solution.py
@@ -357,9 +357,6 @@
         (2, 3): [lambda: second_stage(2)],
         (3, 0): [lambda: second_stage(3)],
         (4, 0): [lambda: share(0)],
-        (4, 1): [lambda: share(1)],
-        (4, 2): [lambda: share(2)],
-        (4, 3): [lambda: share(3)],
     }
     for step in range(1, 5):
         for chunk in range(CHUNKS):
@@ -375,6 +372,8 @@
 
     wait_second(go_recv)
     send(go_buf.at[odd], go_buf.at[odd], go_send, go_recv, 4, partner)
+    for part in range(1, CHUNKS):
+        share(part)
     wait_sent(out_a, a_send, 0)
     wait_first(go_send)
     wait_second(go_send)

time: 61 us -> 59.9 us (0.982)
  Pallas kernels: 60.2 us -> 59.1 us
    pallas_call x1, Pallas kernels: 58.7 us -> 57.6 us  [on_device(): pl.pallas_call(kernel, name='shampoo', out_shape=(left_out, right_out, ja...]
where the time goes in v6:
time: 59.9 us; the launch traced here: 59.8 us
  Pallas kernels  59.1 us (99%)
  between operations  0.64 us (1%)
    pallas_call x1, Pallas kernels, on_device(): pl.pallas_call(kernel, name='shampoo', out_shape=(left_out, right_out, ja...  57.6 us
    pallas_call x1, Pallas kernels, on_device(): pl.pallas_call(export, name='export', out_shape=(left_out, right_out, jax...  1.48 us

profile of v6, /device:TPU:1, one launch (start us, length us, event | category | flops | bytes accessed | tf_op | source)
XLA Modules:
  0.0 59.8 jit_solution(1737983139344500176)
XLA Ops:
  0.6 57.6 %shampoo.1 = (f32[1,2,512,512]{3,2,1,0:T(8,128)S(1)}, f32[1,2,128,128]{3,2,1,0:T(8,128)S(1)}, f32[2,256,128]{2,1,0:T(8,128)S(1)}) custom-call(s32[2,16]{1,0:T(2,128)} %bitcast.1, bf16[128,1024]{1,0:T(8,128)(2,1)} %acts_hbm.1, bf16[128,256]{1,0:T(8,128)(2,1)} %go_hbm.1, f32[1,2,512,512]{3,2,1,0:T(8,128)} %left_hbm.1, f32[1,2,128,128]{3,2,1,0:T(8,128)} %right_hbm.1), custom_call_target="tpu_custom_call" | custom-call | tf_op jit(solution)/shard_map/shampoo/pallas_call | solution.py:491
  58.3 1.5 %export.1 = (f32[1,2,512,512]{3,2,1,0:T(8,128)}, f32[1,2,128,128]{3,2,1,0:T(8,128)}, f32[256,256]{1,0:T(8,128)}) custom-call(f32[1,2,512,512]{3,2,1,0:T(8,128)S(1)} %get-tuple-element.6.nl, f32[1,2,128,128]{3,2,1,0:T(8,128)S(1)} %get-tuple-element.7.nr, f32[2,256,128]{2,1,0:T(8,128)S(1)} %get-tuple-element.8.box), custom_call_target="tpu_custom_call" | custom-call | tf_op jit(solution)/shard_map/export/pallas_call | solution.py:533

commit v7 on v6

--- a/solution.py
+++ b/solution.py
@@ -351,8 +351,8 @@
         (1, 1): [lambda: first_stage(2), lambda: level_left(1)],
         (1, 2): [lambda: first_stage(3), level_right],
         (1, 3): [lambda: old(0), lambda: old(1)],
-        (2, 0): [lambda: old(2), make_tables],
-        (2, 1): [lambda: old(3)],
+        (2, 0): [lambda: old(2), lambda: old(3)],
+        (2, 1): [make_tables],
         (2, 2): [lambda: wait_first(go_recv), lambda: second_stage(1)],
         (2, 3): [lambda: second_stage(2)],
         (3, 0): [lambda: second_stage(3)],

time: 59.9 us -> 59.6 us (level)
  no operation moved by 1% of the time
where the time goes in v7:
time: 59.6 us; the launch traced here: 59.5 us
  Pallas kernels  58.8 us (99%)
  between operations  0.64 us (1%)
    pallas_call x1, Pallas kernels, on_device(): pl.pallas_call(kernel, name='shampoo', out_shape=(left_out, right_out, ja...  57.3 us
    pallas_call x1, Pallas kernels, on_device(): pl.pallas_call(export, name='export', out_shape=(left_out, right_out, jax...  1.48 us

profile of v7, /device:TPU:1, one launch (start us, length us, event | category | flops | bytes accessed | tf_op | source)
XLA Modules:
  0.0 59.5 jit_solution(10982214892345634753)
XLA Ops:
  0.6 57.3 %shampoo.1 = (f32[1,2,512,512]{3,2,1,0:T(8,128)S(1)}, f32[1,2,128,128]{3,2,1,0:T(8,128)S(1)}, f32[2,256,128]{2,1,0:T(8,128)S(1)}) custom-call(s32[2,16]{1,0:T(2,128)} %bitcast.1, bf16[128,1024]{1,0:T(8,128)(2,1)} %acts_hbm.1, bf16[128,256]{1,0:T(8,128)(2,1)} %go_hbm.1, f32[1,2,512,512]{3,2,1,0:T(8,128)} %left_hbm.1, f32[1,2,128,128]{3,2,1,0:T(8,128)} %right_hbm.1), custom_call_target="tpu_custom_call" | custom-call | tf_op jit(solution)/shard_map/shampoo/pallas_call | solution.py:491
  58.0 1.5 %export.1 = (f32[1,2,512,512]{3,2,1,0:T(8,128)}, f32[1,2,128,128]{3,2,1,0:T(8,128)}, f32[256,256]{1,0:T(8,128)}) custom-call(f32[1,2,512,512]{3,2,1,0:T(8,128)S(1)} %get-tuple-element.6.nl, f32[1,2,128,128]{3,2,1,0:T(8,128)S(1)} %get-tuple-element.7.nr, f32[2,256,128]{2,1,0:T(8,128)S(1)} %get-tuple-element.8.box), custom_call_target="tpu_custom_call" | custom-call | tf_op jit(solution)/shard_map/export/pallas_call | solution.py:533
